TPU v7x, 512 devices: a whole 4x8x8 slice. The times are simulated.
512 devices in a mesh: seq: 16 (over z, core), pipe: 32 (over y, x).
Axes of the slice: x: 4, y: 8, z: 8, core: 2. Of those that a mesh axis runs over, the one named last changes fastest.
Arguments:
- projected: bfloat16 [32, 3, 2048, 4096], P('pipe', None, 'seq'), may hold values from -6 to 6
- short_filter: float32 [32, 3, 3, 4096], P('pipe'), may hold values from -3.5 to 3.5
- decay_rate: float32 [32, 16, 4096], P('pipe'), as said below
- residue: float32 [32, 16, 4096], P('pipe'), may hold values from -1.5 to 1.5
- skip_gain: float32 [32, 4096], P('pipe'), may hold values from -4 to 4
Outputs:
- handed: bfloat16 [32, 2048, 4096], P('pipe', 'seq')
Inputs may be any that keep to these rules, and one draw needn't show every extreme that they name: `decay_rate`: every rate lies between 0.2 and 64.
All inputs are finite; a program needn't handle non-finite values.
Results may differ from a plain program's by a relative error of at most 0.01.
Values may be sent and summed in bfloat16 or wider, within the bound.
No kernel may reach another device: no remote copies, remote signals or barrier semaphores. Data moves between devices by JAX's collectives and lax.ppermute only.
A program may use at most 128 MiB of HBM per device.

v0:
```python
import math

import jax
import jax.numpy as jnp
from jax import lax
from jax.sharding import PartitionSpec as P

TAPS = 3


highest = lax.Precision.HIGHEST


def shifted(shard, axis, by):
    size = lax.axis_size(axis)
    pairs = [(i, i + by) for i in range(size) if 0 <= i + by < size]
    return lax.ppermute(shard, axis, pairs)


def response(decay, weight, frequency, support):
    modulus = 2 * support
    folded = (frequency % modulus).astype(jnp.float32)
    parity = (1 - 2 * (frequency % 2)).astype(jnp.float32)
    half_sine = jnp.sin(math.pi * folded / modulus)
    half_square = half_sine * half_sine
    full_sine = jnp.sin(2.0 * math.pi * folded / modulus)
    total_real = None
    total_imag = None
    for mode_index in range(decay.shape[0]):
        rate = decay[mode_index]
        lambda_step = jnp.exp(-rate)
        gap_one = -jnp.expm1(-rate)
        tail_end = jnp.exp(-rate * support)
        real_term = gap_one + 2.0 * lambda_step * half_square
        imag_term = lambda_step * full_sine
        denominator = gap_one * gap_one + 4.0 * lambda_step * half_square
        factor = weight[mode_index] * (1.0 - tail_end * parity) / denominator
        if total_real is None:
            total_real = factor * real_term
            total_imag = -factor * imag_term
        else:
            total_real = total_real + factor * real_term
            total_imag = total_imag - factor * imag_term
    return (total_real, total_imag)


def angle_table(first, second, modulus):
    return 2.0 * math.pi * (first * second % modulus).astype(jnp.float32) / modulus


def spectral_mix(gated, decay, scaled, nseq, length, total):
    width = gated.shape[1]
    share = width // nseq
    spread = lax.all_to_all(gated, "seq", split_axis=1, concat_axis=0, tiled=True)
    spread = spread.reshape(nseq, length, share)
    start = lax.axis_index("seq") * share
    decay_mine = lax.dynamic_slice_in_dim(decay, start, share, 1)
    scaled_mine = lax.dynamic_slice_in_dim(scaled, start, share, 1)
    block = math.gcd(share, 128)
    count = share // block
    double = 2 * nseq
    modulus = 2 * total
    outer_freq = jnp.arange(double, dtype=jnp.int32)
    device_pos = jnp.arange(nseq, dtype=jnp.int32)
    token_pos = jnp.arange(length, dtype=jnp.int32)
    outer_angle = angle_table(outer_freq[:, None], device_pos[None, :], double)
    outer_cos = jnp.cos(outer_angle)
    outer_sin = jnp.sin(outer_angle)
    twist_angle = angle_table(outer_freq[:, None], token_pos[None, :], modulus)[:, :, None]
    twist_cos = jnp.cos(twist_angle)
    twist_sin = jnp.sin(twist_angle)
    inner_angle = angle_table(token_pos[:, None], token_pos[None, :], length)
    inner_cos = jnp.cos(inner_angle)
    inner_sin = jnp.sin(inner_angle)
    frequency = (outer_freq[:, None] + double * token_pos[None, :])[:, :, None]

    def one_block(block_index, result):
        values = lax.dynamic_slice_in_dim(spread, block_index * block, block, 2).astype(jnp.float32)
        rates = lax.dynamic_slice_in_dim(decay_mine, block_index * block, block, 1)[
            :, None, None, :
        ]
        weights = lax.dynamic_slice_in_dim(scaled_mine, block_index * block, block, 1)[
            :, None, None, :
        ]
        first_real = jnp.einsum("kj,jrc->krc", outer_cos, values, precision=highest)
        first_imag = -jnp.einsum("kj,jrc->krc", outer_sin, values, precision=highest)
        turned_real = first_real * twist_cos + first_imag * twist_sin
        turned_imag = first_imag * twist_cos - first_real * twist_sin
        spec_real = jnp.einsum(
            "qr,krc->kqc", inner_cos, turned_real, precision=highest
        ) + jnp.einsum("qr,krc->kqc", inner_sin, turned_imag, precision=highest)
        spec_imag = jnp.einsum(
            "qr,krc->kqc", inner_cos, turned_imag, precision=highest
        ) - jnp.einsum("qr,krc->kqc", inner_sin, turned_real, precision=highest)
        gain_real, gain_imag = response(rates, weights, frequency, total)
        prod_real = spec_real * gain_real - spec_imag * gain_imag
        prod_imag = spec_real * gain_imag + spec_imag * gain_real
        back_real = jnp.einsum("qr,kqc->krc", inner_cos, prod_real, precision=highest) - jnp.einsum(
            "qr,kqc->krc", inner_sin, prod_imag, precision=highest
        )
        back_imag = jnp.einsum("qr,kqc->krc", inner_cos, prod_imag, precision=highest) + jnp.einsum(
            "qr,kqc->krc", inner_sin, prod_real, precision=highest
        )
        reverted_real = back_real * twist_cos - back_imag * twist_sin
        reverted_imag = back_imag * twist_cos + back_real * twist_sin
        mixed_block = (
            jnp.einsum("kj,krc->jrc", outer_cos, reverted_real, precision=highest)
            - jnp.einsum("kj,krc->jrc", outer_sin, reverted_imag, precision=highest)
        ) / modulus
        return lax.dynamic_update_slice_in_dim(result, mixed_block, block_index * block, 2)

    mixed = lax.fori_loop(0, count, one_block, jnp.zeros((nseq, length, share), jnp.float32))
    return lax.all_to_all(
        mixed.reshape(total, share), "seq", split_axis=0, concat_axis=1, tiled=True
    )


def shards(projected, short_filter, decay_rate, residue, skip_gain):
    length = projected.shape[2]
    nseq = lax.axis_size("seq")
    total = length * nseq
    rim_part = projected[:, :, length - (TAPS - 1) :, :]
    before = shifted(rim_part, "seq", 1)
    extended = jnp.concatenate([before, projected], axis=2).astype(jnp.float32)
    featured = short_filter[:, :, 0, None, :] * extended[:, :, TAPS - 1 : TAPS - 1 + length, :]
    for offset in range(1, TAPS):
        featured = (
            featured
            + short_filter[:, :, offset, None, :]
            * extended[:, :, TAPS - 1 - offset : TAPS - 1 - offset + length, :]
        )
    gated = (featured[0, 1] * featured[0, 2]).astype(jnp.bfloat16)
    decay = decay_rate[0] / total
    scaled = residue[0] * jnp.sqrt(-jnp.expm1(-2.0 * decay))
    mixed = spectral_mix(gated, decay, scaled, nseq, length, total)
    output = (featured[0, 0] * (mixed + skip_gain[0] * gated.astype(jnp.float32))).astype(
        jnp.bfloat16
    )
    return shifted(output[None], "pipe", 1)


def solution(mesh):
    in_specs = (
        P("pipe", None, "seq", None),
        P("pipe", None, None, None),
        P("pipe", None, None),
        P("pipe", None, None),
        P("pipe", None),
    )
    out_specs = P("pipe", "seq", None)
    return jax.shard_map(shards, mesh=mesh, in_specs=in_specs, out_specs=out_specs, check_vma=False)
```

profile of v0, /device:TPU:32, one launch (start us, length us, event | category | flops | bytes accessed | tf_op | source)
XLA Modules:
  0.0 282.4 jit_solution(17337421836262055718)
XLA Ops:
  3.7 3.5 %copy.48 = bf16[1,3,128,4096]{2,3,1,0:T(8,128)(2,1)S(1)} copy(bf16[1,3,128,4096]{3,2,1,0:T(8,128)(2,1)} %param.7) | data formatting | bytes 6291456 | tf_op args[0]
  7.2 2.8 %copy.47 = bf16[1,3,2,4096]{2,3,1,0:T(8,128)(2,1)} copy(bf16[1,3,2,4096]{3,2,1,0:T(2,128)(2,1)S(1)} %collective-permute-done) | data formatting | bytes 98304 | tf_op jit(solution)/shard_map/ppermute | solution.py:17
  10.1 4.1 %maximum_convert_fusion = f32[1,3,130,4096]{2,3,1,0:T(8,128)S(1)} fusion(bf16[1,3,128,4096]{2,3,1,0:T(8,128)(2,1)S(1)} %copy.48, bf16[1,3,2,4096]{2,3,1,0:T(8,128)(2,1)} %copy.47), kind=kLoop, calls=%fused_computation.301 | loop fusion | flops 6389760 | bytes 9584640 | tf_op jit(solution)/shard_map/convert_element_type | solution.py:124
  14.1 9.4 %fusion.133 = f32[1,3,128,4096]{2,3,1,0:T(8,128)S(1)} fusion(f32[1,3,130,4096]{2,3,1,0:T(8,128)S(1)} %maximum_convert_fusion, f32[3,4096]{1,0:T(4,128)S(1)} %get-tuple-element.1313, f32[3,4096]{1,0:T(4,128)S(1)} %get-tuple-element.1314, f32[3,4096]{1,0:T(4,128)S(1)} %bitcast.462), kind=kLoop, calls=%fused_computation.297 | loop fusion | flops 7864320 | bytes 25313280 | tf_op jit(solution)/shard_map/add | solution.py:128
  23.5 2.6 copy-done.1
  27.7 11.8 %all-to-all-start = ((bf16[128,16,256]{2,0,1:T(8,128)(2,1)}), bf16[128,16,256]{2,0,1:T(8,128)(2,1)S(1)}, u32[]{:S(2)}, u32[]{:S(2)}) async-start(bf16[128,16,256]{2,0,1:T(8,128)(2,1)} %copy.49), calls=%async_computation | async-start | bytes 2097152 | tf_op jit(solution)/shard_map/all_to_all | solution.py:54
  40.2 25.9 %all-to-all-done = bf16[128,16,256]{2,0,1:T(8,128)(2,1)S(1)} async-done(((bf16[128,16,256]{2,0,1:T(8,128)(2,1)}), bf16[128,16,256]{2,0,1:T(8,128)(2,1)S(1)}, u32[]{:S(2)}, u32[]{:S(2)}) %all-to-all-start) | async-done | bytes 1048608 | tf_op jit(solution)/shard_map/all_to_all | solution.py:54
  67.7 122.1 %while.21 = (s32[]{:T(128)}, f32[16,128,256]{2,1,0:T(8,128)}, bf16[16,128,256]{2,1,0:T(8,128)(2,1)S(1)}, f32[16,256]{1,0:T(8,128)S(1)}, f32[16,256]{1,0:T(8,128)...) while((s32[]{:T(128)}, f32[16,128,256]{2,1,0:T(8,128)}, ...), condition=%wide.region_1.2_spmd.clone.clone.clone, body=%wide.region_0.1_spmd.clone.clone.clone.sunk | while | flops 6968283136 | bytes 135685840 | solution.py:112
  70.4 4.0 %fusion.209 = (f32[32,128,128]{2,0,1:T(8,128)S(1)}, f32[32,128,128]{2,0,1:T(8,128)}) fusion(f32[128,128,32]{1,2,0:T(8,128)S(1)} %fusion.208, f32[32,128]{0,1:T(8,128)S(1)} %get-tuple-element.1492, f32[32,128]{0,1:T(8,128)S(1)} %get-tuple-element.1493, bf16[16,128,128]{2,1,0:T(8,128)(2,1)S(1)} %constant_dynamic-slice_fusion.4), kind=kOutput, calls=%fused_computation.16.clone.1 | convolution fusion | flops 104340480 | bytes 6848512 | tf_op jit(solution)/shard_map/while/body/eval_jaxpr/kj,jrc->krc/dot_general | solution.py:85
  76.2 2.3 copy.84
  78.5 2.1 fusion.213
  82.8 2.1 convolution_add_fusion.4
  84.9 19.1 %fusion.214 = (f32[32,128,128]{1,2,0:T(8,128)S(1)}, f32[32,128,128]{1,2,0:T(8,128)S(1)}, f32[32,128,128]{1,2,0:T(8,128)S(1)}, f32[32,128,128]{2,1,0:T(8,128)S(1)}) fusion(f32[32,128,128]{2,1,0:T(8,128)S(1)} %convolution_add_fusion.4, f32[128]{0:T(128)S(1)} %get-tuple-element.1496, f32[128]{0:T(128)S(1)} %get-tuple-element.1499, ...), kind=kOutput, calls=%fused_computation.10.clone.1 | convolution fusion | flops 916160512 | bytes 14786560 | tf_op jit(solution)/shard_map/while/body/eval_jaxpr/qr,krc->kqc/dot_general | solution.py:94
  105.0 2.1 fusion.216
  111.4 3.8 %add_bitcast_fusion.2 = (f32[32,128,128]{1,2,0:T(8,128)S(1)}, f32[32,128,128]{1,2,0:T(8,128)}) fusion(f32[32,128,128]{2,1,0:T(8,128)S(1)} %convolution_add_fusion.5, f32[32,128]{1,0:T(8,128)S(1)} %copy.85, f32[32,128]{1,0:T(8,128)S(1)} %copy.86, f32[32,128,128]{2,1,0:T(8,128)S(1)} %fusion.217, f32[32,128,128]{1,2,0:T(8,128)S(1)} %fusion.215), kind=kOutput, calls=%fused_computation.20.clone.1 | convolution fusion | flops 809205760 | bytes 10518528 | tf_op jit(solution)/shard_map/while/body/eval_jaxpr/qr,kqc->krc/dot_general | solution.py:98
  115.2 3.1 %copy.87 = f32[32,128,128]{2,0,1:T(8,128)} copy(f32[32,128,128]{1,2,0:T(8,128)} %get-tuple-element.1630) | data formatting | bytes 4194304 | tf_op jit(solution)/shard_map/while/body/eval_jaxpr/sub | solution.py:104
  118.2 2.8 %fusion.218 = f32[128,128,16]{1,2,0:T(8,128)S(1)} fusion(f32[32,128,128]{2,0,1:T(8,128)} %copy.87), kind=kOutput, calls=%fused_computation.109.clone.1 | convolution fusion | flops 100670464 | bytes 3145728 | tf_op jit(solution)/shard_map/while/body/eval_jaxpr/kj,krc->jrc/dot_general | solution.py:107
  123.1 3.0 %fusion.219 = f32[16,128,128]{2,0,1:T(8,128)S(1)} fusion(f32[128,128,16]{1,2,0:T(8,128)S(1)} %fusion.218, f32[32,128,128]{2,0,1:T(8,128)} %copy.88), kind=kOutput, calls=%fused_computation.46.clone.1 | convolution fusion | flops 101194752 | bytes 4194304 | tf_op jit(solution)/shard_map/while/body/eval_jaxpr/kj,krc->jrc/dot_general | solution.py:108
  130.6 4.0 %fusion.209 = (f32[32,128,128]{2,0,1:T(8,128)S(1)}, f32[32,128,128]{2,0,1:T(8,128)}) fusion(f32[128,128,32]{1,2,0:T(8,128)S(1)} %fusion.208, f32[32,128]{0,1:T(8,128)S(1)} %get-tuple-element.1492, f32[32,128]{0,1:T(8,128)S(1)} %get-tuple-element.1493, bf16[16,128,128]{2,1,0:T(8,128)(2,1)S(1)} %constant_dynamic-slice_fusion.4), kind=kOutput, calls=%fused_computation.16.clone.1 | convolution fusion | flops 104340480 | bytes 6848512 | tf_op jit(solution)/shard_map/while/body/eval_jaxpr/kj,jrc->krc/dot_general | solution.py:85
  136.4 2.4 copy.84
  138.8 2.1 fusion.213
  143.1 2.1 convolution_add_fusion.4
  145.3 18.7 %fusion.214 = (f32[32,128,128]{1,2,0:T(8,128)S(1)}, f32[32,128,128]{1,2,0:T(8,128)S(1)}, f32[32,128,128]{1,2,0:T(8,128)S(1)}, f32[32,128,128]{2,1,0:T(8,128)S(1)}) fusion(f32[32,128,128]{2,1,0:T(8,128)S(1)} %convolution_add_fusion.4, f32[128]{0:T(128)S(1)} %get-tuple-element.1496, f32[128]{0:T(128)S(1)} %get-tuple-element.1499, ...), kind=kOutput, calls=%fused_computation.10.clone.1 | convolution fusion | flops 916160512 | bytes 14786560 | tf_op jit(solution)/shard_map/while/body/eval_jaxpr/qr,krc->kqc/dot_general | solution.py:94
  165.0 2.1 fusion.216
  171.4 3.8 %add_bitcast_fusion.2 = (f32[32,128,128]{1,2,0:T(8,128)S(1)}, f32[32,128,128]{1,2,0:T(8,128)}) fusion(f32[32,128,128]{2,1,0:T(8,128)S(1)} %convolution_add_fusion.5, f32[32,128]{1,0:T(8,128)S(1)} %copy.85, f32[32,128]{1,0:T(8,128)S(1)} %copy.86, f32[32,128,128]{2,1,0:T(8,128)S(1)} %fusion.217, f32[32,128,128]{1,2,0:T(8,128)S(1)} %fusion.215), kind=kOutput, calls=%fused_computation.20.clone.1 | convolution fusion | flops 809205760 | bytes 10518528 | tf_op jit(solution)/shard_map/while/body/eval_jaxpr/qr,kqc->krc/dot_general | solution.py:98
  175.2 3.1 %copy.87 = f32[32,128,128]{2,0,1:T(8,128)} copy(f32[32,128,128]{1,2,0:T(8,128)} %get-tuple-element.1630) | data formatting | bytes 4194304 | tf_op jit(solution)/shard_map/while/body/eval_jaxpr/sub | solution.py:104
  178.2 2.8 %fusion.218 = f32[128,128,16]{1,2,0:T(8,128)S(1)} fusion(f32[32,128,128]{2,0,1:T(8,128)} %copy.87), kind=kOutput, calls=%fused_computation.109.clone.1 | convolution fusion | flops 100670464 | bytes 3145728 | tf_op jit(solution)/shard_map/while/body/eval_jaxpr/kj,krc->jrc/dot_general | solution.py:107
  183.1 3.0 %fusion.219 = f32[16,128,128]{2,0,1:T(8,128)S(1)} fusion(f32[128,128,16]{1,2,0:T(8,128)S(1)} %fusion.218, f32[32,128,128]{2,0,1:T(8,128)} %copy.88), kind=kOutput, calls=%fused_computation.46.clone.1 | convolution fusion | flops 101194752 | bytes 4194304 | tf_op jit(solution)/shard_map/while/body/eval_jaxpr/kj,krc->jrc/dot_general | solution.py:108
  189.8 54.5 %all_to_all.29 = f32[16,128,256]{2,1,0:T(8,128)S(1)} all-to-all(f32[16,128,256]{2,1,0:T(8,128)} %get-tuple-element.836), channel_id=1, replica_groups=mesh['seq'=16,'pipe'=32] {'seq'}, dimensions={0} | all-to-all | bytes 4194304 | tf_op jit(solution)/shard_map/all_to_all | solution.py:113
  246.3 3.8 %fusion.137 = bf16[1,128,4096]{1,2,0:T(8,128)(2,1)S(1)} fusion(f32[1,3,128,4096]{2,3,1,0:T(8,128)} %copy-done.1, f32[4096]{0:T(1024)S(1)} %bitcast.463, f32[1,128,4096]{1,2,0:T(8,128)} %bitcast.460), kind=kLoop, calls=%fused_computation.306 | loop fusion | flops 3670016 | bytes 9453568 | tf_op jit(solution)/shard_map/convert_element_type | solution.py:136
  250.1 3.4 %collective-permute-start.1 = (bf16[1,128,4096]{1,2,0:T(8,128)(2,1)S(1)}, bf16[1,128,4096]{1,2,0:T(8,128)(2,1)S(1)}, u32[]{:S(2)}, u32[]{:S(2)}) collective-permute-start(bf16[1,128,4096]{1,2,0:T(8,128)(2,1)S(1)} %fusion.137), channel_id=1, source_target_pairs={{0,1},{1,2},{2,3},{3,4},{4,5},{5,6},{6,7},{7,8},{8,9},{9,10},{10,1... | collective-permute-start | bytes 3145736 | tf_op jit(solution)/shard_map/ppermute | solution.py:17
  253.5 27.2 %collective-permute-done.1 = bf16[1,128,4096]{1,2,0:T(8,128)(2,1)S(1)} collective-permute-done((bf16[1,128,4096]{1,2,0:T(8,128)(2,1)S(1)}, bf16[1,128,4096]{1,2,0:T(8,128)(2,1)S(1)}, u32[]{:S(2)}, u32[]{:S(2)}) %collective-permute-start.1) | collective-permute-done | bytes 1048608 | tf_op jit(solution)/shard_map/ppermute | solution.py:17
  (100 shorter events, 41.4 us)
Async XLA Ops:
  1.0 6.2 %collective-permute-start = (bf16[1,3,2,4096]{3,2,1,0:T(2,128)(2,1)S(1)}, bf16[1,3,2,4096]{3,2,1,0:T(2,128)(2,1)S(1)}, u32[]{:S(2)}, u32[]{:S(2)}) collective-permute-start(bf16[1,3,2,4096]{3,2,1,0:T(2,128)(2,1)S(1)} %slice.479), channel_id=1, source_target_pairs={{0,32},{32,64},{64,96},{96,128},{128,160},{160,192},{192,224},{224... | collective-permute-start | bytes 147464 | tf_op jit(solution)/shard_map/ppermute | solution.py:17
  23.5 2.6 copy-start.1
  27.7 38.4 %all-to-all-start = ((bf16[128,16,256]{2,0,1:T(8,128)(2,1)}), bf16[128,16,256]{2,0,1:T(8,128)(2,1)S(1)}, u32[]{:S(2)}, u32[]{:S(2)}) async-start(bf16[128,16,256]{2,0,1:T(8,128)(2,1)} %copy.49), calls=%async_computation | async-start | bytes 2097152 | tf_op jit(solution)/shard_map/all_to_all | solution.py:54
  67.9 1.3 copy-start.2
  78.5 2.2 copy-start
  123.1 3.0 %copy-start.4 = (f32[16,128,256]{2,1,0:T(8,128)S(1)}, f32[16,128,256]{2,1,0:T(8,128)}, u32[]{:S(2)}) copy-start(f32[16,128,256]{2,1,0:T(8,128)} %get-tuple-element.1658) | copy-start | bytes 6291460 | tf_op jit(solution)/shard_map/while
  126.1 1.9 copy-start.3
  126.5 1.4 copy-start.5
  128.1 1.3 copy-start.2
  138.8 2.2 copy-start
  183.1 3.0 %copy-start.4 = (f32[16,128,256]{2,1,0:T(8,128)S(1)}, f32[16,128,256]{2,1,0:T(8,128)}, u32[]{:S(2)}) copy-start(f32[16,128,256]{2,1,0:T(8,128)} %get-tuple-element.1658) | copy-start | bytes 6291460 | tf_op jit(solution)/shard_map/while
  186.1 1.9 copy-start.3
  186.5 1.4 copy-start.5
  244.4 1.9 copy-start.6
  250.1 30.6 %collective-permute-start.1 = (bf16[1,128,4096]{1,2,0:T(8,128)(2,1)S(1)}, bf16[1,128,4096]{1,2,0:T(8,128)(2,1)S(1)}, u32[]{:S(2)}, u32[]{:S(2)}) collective-permute-start(bf16[1,128,4096]{1,2,0:T(8,128)(2,1)S(1)} %fusion.137), channel_id=1, source_target_pairs={{0,1},{1,2},{2,3},{3,4},{4,5},{5,6},{6,7},{7,8},{8,9},{9,10},{10,1... | collective-permute-start | bytes 3145736 | tf_op jit(solution)/shard_map/ppermute | solution.py:17
where the time goes:
time: 288 us; the launch traced here: 282 us
  matrix products  92.6 us (32%)
  blocking collectives  54.5 us (19%)
  waiting for transfers between devices  53 us (18%)
  local copies, waits for them, and re-layouts  40.2 us (14%)
  other arithmetic  21.6 us (8%)
  starting transfers between devices  16.9 us (6%)
  loops' own time  2.92 us (1%)
    all_to_all x1, blocking collectives, spectral_mix(): lax.all_to_all(mixed.reshape(total, share), 'seq', split_axis=0, concat_a...  54.5 us
    dot_general x2, matrix products, one_block(): jnp.einsum('qr,krc->kqc', inner_sin, turned_real, precision=highest)  37.8 us
    ppermute x2, waiting for transfers between devices, shifted(): return lax.ppermute(shard, axis, pairs)  27.2 us
    all_to_all x1, waiting for transfers between devices, spectral_mix(): lax.all_to_all(gated, 'seq', split_axis=1, concat_axis=0, tiled=True)  25.9 us
    all_to_all x1, starting transfers between devices, spectral_mix(): lax.all_to_all(gated, 'seq', split_axis=1, concat_axis=0, tiled=True)  11.8 us
    add x1, other arithmetic, shards(): featured + short_filter[:, :, offset, None, :] * extended[:, :, TAPS - 1...  9.39 us
    dot_general x2, matrix products, one_block(): first_real = jnp.einsum('kj,jrc->krc', outer_cos, values, precision=highest)  7.92 us
    dot_general x2, matrix products, one_block(): jnp.einsum('qr,kqc->krc', inner_sin, prod_imag, precision=highest)  7.59 us
  transfers between devices with their start and end apart: 3, of which 2 were waited for; matrix products, arithmetic and copies ran while one was open for 2% of the time, Pallas kernels for 0%

commit v1 on v0

v1 whole, which is shorter than its diff:
```python
import functools

import jax
import jax.numpy as jnp
from jax import lax
from jax.experimental import pallas as pl
from jax.experimental.pallas import tpu as pltpu
from jax.sharding import PartitionSpec as P

TAPS = 3
LANES = 128
ROWS = 8
GROUP = ROWS * LANES


def spread_rows(dst, base, pitch, value):
    n = value.shape[0]
    for k in range(ROWS):
        dst[pl.ds(base + k * pitch, n), :] = value[:, k * LANES : (k + 1) * LANES]


def state_kernel(order, length, pitch, total,
                 inputs, rim, taps, rates, end_ref, span_ref, lead_ref, gate_ref,
                 raw, tap_rows, rate_rows):
    f32 = jnp.float32
    for i in range(3):
        for k in range(ROWS):
            lanes = pl.ds(k * LANES, LANES)
            raw[i, pl.ds(k * pitch + 8, length), :] = inputs[0, i, :, lanes].astype(f32)
            raw[i, pl.ds(k * pitch + 8 - (TAPS - 1), TAPS - 1), :] = rim[0, i, :, lanes].astype(f32)
        for a in range(TAPS):
            for k in range(ROWS):
                tap_rows[i, a, pl.ds(k, 1), :] = taps[0, i, pl.ds(a, 1), pl.ds(k * LANES, LANES)]
    for k in range(ROWS):
        rate_rows[pl.ds(k * order, order), :] = rates[0, :, pl.ds(k * LANES, LANES)]

    def token(i, t):
        return raw[i, pl.ds(8 + t, ROWS, stride=pitch), :]

    weights = [[tap_rows[i, a] for a in range(TAPS)] for i in range(3)]

    def feature_step(t, before):
        after = []
        made = []
        for i in range(3):
            now = token(i, t)
            one, two = before[i]
            made.append(weights[i][0] * now + weights[i][1] * one + weights[i][2] * two)
            after.append((now, one))
        lead_ref[0, t] = made[0]
        gate_ref[0, t] = (made[1] * made[2]).astype(jnp.bfloat16).astype(f32)
        return tuple(after)

    lax.fori_loop(0, length, feature_step,
                  tuple((token(i, -1), token(i, -2)) for i in range(3)), unroll=8)

    steps = []
    for n in range(order):
        rate = rate_rows[pl.ds(n, ROWS, stride=order), :]
        span_ref[0, n] = rate * (length / total)
        steps.append(jnp.exp(-(rate / total)))

    def state_step(t, states):
        gated = gate_ref[0, t]
        return tuple(s * x + gated for s, x in zip(steps, states))

    zero = jnp.zeros((ROWS, LANES), f32)
    states = lax.fori_loop(0, length, state_step, (zero,) * order, unroll=4)
    for n in range(order):
        end_ref[0, n] = states[n]


def output_kernel(order, length, pitch, total,
                  lead, gate, rates, scaled, skip, start, out_ref,
                  rows, rate_rows, scale_rows, skip_rows):
    for k in range(ROWS):
        lanes = pl.ds(k * LANES, LANES)
        rate_rows[pl.ds(k * order, order), :] = rates[0, :, lanes]
        scale_rows[pl.ds(k * order, order), :] = scaled[:, lanes]
        skip_rows[pl.ds(k, 1), :] = skip[:, lanes]
    steps, scales = [], []
    for n in range(order):
        steps.append(jnp.exp(-(rate_rows[pl.ds(n, ROWS, stride=order), :] / total)))
        scales.append(scale_rows[pl.ds(n, ROWS, stride=order), :])

    def mix_step(t, states):
        gated = gate[0, t]
        states = tuple(s * x + gated for s, x in zip(steps, states))
        parts = [w * x for w, x in zip(scales, states)]
        while len(parts) > 1:
            parts = [parts[i] + parts[i + 1] for i in range(0, len(parts), 2)]
        made = lead[0, t] * (parts[0] + skip_rows[...] * gated)
        rows[pl.ds(t, ROWS, stride=pitch), :] = made
        return states

    lax.fori_loop(0, length, mix_step, tuple(start[0, n] for n in range(order)), unroll=2)
    for k in range(ROWS):
        out_ref[0, :, pl.ds(k * LANES, LANES)] = rows[pl.ds(k * pitch, length), :].astype(jnp.bfloat16)


def local_states(projected, rim, short_filter, decay_rate, total):
    length, width = projected.shape[2:]
    order = decay_rate.shape[1]
    groups = width // GROUP
    pitch = length + 8
    f32 = jnp.float32
    whole = lambda n: pl.BlockSpec((1, n, ROWS, LANES), lambda g: (g, 0, 0, 0))
    shape = lambda n: jax.ShapeDtypeStruct((groups, n, ROWS, LANES), f32)
    return pl.pallas_call(
        functools.partial(state_kernel, order, length, pitch, total),
        grid=(groups,),
        in_specs=[
            pl.BlockSpec((1, 3, length, GROUP), lambda g: (0, 0, 0, g)),
            pl.BlockSpec((1, 3, TAPS - 1, GROUP), lambda g: (0, 0, 0, g)),
            pl.BlockSpec((1, 3, TAPS, GROUP), lambda g: (0, 0, 0, g)),
            pl.BlockSpec((1, order, GROUP), lambda g: (0, 0, g)),
        ],
        out_specs=[whole(order), whole(order), whole(length), whole(length)],
        out_shape=[shape(order), shape(order), shape(length), shape(length)],
        scratch_shapes=[
            pltpu.VMEM((3, ROWS * pitch, LANES), f32),
            pltpu.VMEM((3, TAPS, ROWS, LANES), f32),
            pltpu.VMEM((ROWS * order, LANES), f32),
        ],
        compiler_params=pltpu.CompilerParams(vmem_limit_bytes=24 << 20),
        name="local_states",
    )(projected, rim, short_filter, decay_rate)


def mixed_output(lead, gate, decay_rate, scaled, skip_gain, start, total):
    groups, length = lead.shape[:2]
    order = decay_rate.shape[1]
    pitch = length
    f32 = jnp.float32
    whole = lambda n: pl.BlockSpec((1, n, ROWS, LANES), lambda g: (g, 0, 0, 0))
    return pl.pallas_call(
        functools.partial(output_kernel, order, length, pitch, total),
        grid=(groups,),
        in_specs=[
            whole(length),
            whole(length),
            pl.BlockSpec((1, order, GROUP), lambda g: (0, 0, g)),
            pl.BlockSpec((order, GROUP), lambda g: (0, g)),
            pl.BlockSpec((1, GROUP), lambda g: (0, g)),
            whole(order),
        ],
        out_specs=pl.BlockSpec((1, length, GROUP), lambda g: (0, 0, g)),
        out_shape=jax.ShapeDtypeStruct((1, length, groups * GROUP), jnp.bfloat16),
        scratch_shapes=[
            pltpu.VMEM((ROWS * pitch, LANES), f32),
            pltpu.VMEM((ROWS * order, LANES), f32),
            pltpu.VMEM((ROWS * order, LANES), f32),
            pltpu.VMEM((ROWS, LANES), f32),
        ],
        compiler_params=pltpu.CompilerParams(vmem_limit_bytes=24 << 20),
        name="mixed_output",
    )(lead, gate, decay_rate, scaled, skip_gain, start)


def moved(x, pairs):
    return lax.ppermute(x, "seq", pairs)


def prefix(ends, span):
    nseq = lax.axis_size("seq")
    chips = nseq // 2
    me = lax.axis_index("seq")
    core, chip = me % 2, me // 2
    half = ends.shape[1] // 2
    first = core == 0
    low = lambda x: x[:, :half]
    high = lambda x: x[:, half:]
    mine = lambda x: jnp.where(first, low(x), high(x))
    others = lambda x: jnp.where(first, high(x), low(x))
    swap = [(i, i ^ 1) for i in range(nseq)]
    own, came = mine(ends), moved(others(ends), swap)
    span = mine(span)
    zeroth, oneth = jnp.where(first, own, came), jnp.where(first, came, own)
    fade = jnp.exp(-span)
    whole = fade * zeroth + oneth
    enter = None
    step = 1
    while step < chips // 2:
        came = moved(whole, [(i, ((i // 2) ^ step) * 2 + i % 2) for i in range(nseq)])
        right = (chip & step) != 0
        far = jnp.exp(-span * (2 * (chip & (step - 1))).astype(jnp.float32))
        into = jnp.where(right, far * came, 0.0)
        enter = into if enter is None else enter + into
        fading = jnp.exp(-span * (2.0 * step))
        whole = jnp.where(right, fading * came + whole, fading * whole + came)
        step *= 2
    came = moved(whole, [(c * 2 + k, (chips - 1 - c) * 2 + k) for c in range(chips // 2) for k in range(2)])
    far = jnp.exp(-span * (2 * (chip & (step - 1))).astype(jnp.float32))
    enter = enter + far * came
    second = fade * enter + zeroth
    came = moved(jnp.where(first, second, enter), swap)
    own = jnp.where(first, enter, second)
    return jnp.concatenate([jnp.where(first, own, came), jnp.where(first, came, own)], axis=1)


def shards(projected, short_filter, decay_rate, residue, skip_gain):
    length = projected.shape[2]
    nseq = lax.axis_size("seq")
    total = length * nseq
    edge = projected[:, :, length - (TAPS - 1) :, :]
    rim = moved(edge, [(i, i + 1) for i in range(nseq - 1)])
    ends, span, lead, gate = local_states(projected, rim, short_filter, decay_rate, total)
    scaled = residue[0] * jnp.sqrt(-jnp.expm1(-2.0 * (decay_rate[0] / total)))
    start = prefix(ends, span)
    output = mixed_output(lead, gate, decay_rate, scaled, skip_gain, start, total)
    sections = lax.axis_size("pipe")
    return lax.ppermute(output, "pipe", [(i, i + 1) for i in range(sections - 1)])


def solution(mesh):
    in_specs = (
        P("pipe", None, "seq", None),
        P("pipe", None, None, None),
        P("pipe", None, None),
        P("pipe", None, None),
        P("pipe", None),
    )
    out_specs = P("pipe", "seq", None)
    return jax.shard_map(shards, mesh=mesh, in_specs=in_specs, out_specs=out_specs, check_vma=False)
```

time: 288 us -> 96.3 us (0.33); the launches traced: 282 us -> 95.8 us
  matrix products: 92.6 us -> 0 us
  blocking collectives: 54.5 us -> 0 us
  local copies, waits for them, and re-layouts: 40.2 us -> 7.14 us
  other arithmetic: 21.6 us -> 1.24 us
  starting transfers between devices: 16.9 us -> 30.9 us
  Pallas kernels: 0 us -> 12.3 us
  waiting for transfers between devices: 53 us -> 44.1 us
  loops' own time: 2.92 us -> 0 us
    dot_general x24 -> x0, matrix products: 92.6 us -> none  [the longest x2 37.8 us: one_block(): jnp.einsum('qr,krc->kqc', inner_sin, turned_real, precision=highest)]
    all_to_all x1 -> x0, blocking collectives: 54.5 us -> none  [spectral_mix(): lax.all_to_all(mixed.reshape(total, share), 'seq', split_axis=0, concat_a...]
    all_to_all x1 -> x0, waiting for transfers between devices: 25.9 us -> none  [spectral_mix(): lax.all_to_all(gated, 'seq', split_axis=1, concat_axis=0, tiled=True)]
    ppermute x2 -> x7, starting transfers between devices: 5.12 us -> 30.9 us  [the longest x6 27.5 us: moved(): return lax.ppermute(x, 'seq', pairs)]
    ppermute x2 -> x7, waiting for transfers between devices: 27.2 us -> 44.1 us  [the longest x1 27 us: shards(): lax.ppermute(output, 'pipe', [(i, i + 1) for i in range(sections - 1)])]
    pallas_call x0 -> x2, Pallas kernels: none -> 12.3 us  [the longest x1 7.03 us: mixed_output(): pl.pallas_call(functools.partial(output_kernel, order, length, pitch, tot...]
    all_to_all x1 -> x0, starting transfers between devices: 11.8 us -> none  [spectral_mix(): lax.all_to_all(gated, 'seq', split_axis=1, concat_axis=0, tiled=True)]
    add x3 -> x1, other arithmetic: 11.3 us -> 0.05 us  [prefix(): whole = fade * zeroth + oneth]
  transfers between devices with their start and end apart: 3 -> 7, of which waited for: 2 -> 6; matrix products, arithmetic and copies ran while one was open for 2% -> 1% of each run, Pallas kernels for 0% -> 0%
where the time goes in v1:
time: 96.3 us; the launch traced here: 95.8 us
  waiting for transfers between devices  44.1 us (46%)
  starting transfers between devices  30.9 us (32%)
  Pallas kernels  12.3 us (13%)
  local copies, waits for them, and re-layouts  7.14 us (7%)
  other arithmetic  1.24 us (1%)
    ppermute x6, starting transfers between devices, moved(): return lax.ppermute(x, 'seq', pairs)  27.5 us
    ppermute x1, waiting for transfers between devices, shards(): lax.ppermute(output, 'pipe', [(i, i + 1) for i in range(sections - 1)])  27 us
    ppermute x6, waiting for transfers between devices, moved(): return lax.ppermute(x, 'seq', pairs)  17 us
    pallas_call x1, Pallas kernels, mixed_output(): pl.pallas_call(functools.partial(output_kernel, order, length, pitch, tot...  7.03 us
    unnamed x16, local copies, waits for them, and re-layouts  6.16 us
    pallas_call x1, Pallas kernels, local_states(): pl.pallas_call(functools.partial(state_kernel, order, length, pitch, tota...  5.3 us
    ppermute x1, starting transfers between devices, shards(): lax.ppermute(output, 'pipe', [(i, i + 1) for i in range(sections - 1)])  3.4 us
  transfers between devices with their start and end apart: 7, of which 6 were waited for; matrix products, arithmetic and copies ran while one was open for 1% of the time, Pallas kernels for 0%

profile of v1, /device:TPU:32, one launch (start us, length us, event | category | flops | bytes accessed | tf_op | source)
XLA Modules:
  0.0 95.8 jit_solution(12079038688354662695)
XLA Ops:
  0.0 1.0 %slice.17 = bf16[1,3,2,4096]{3,2,1,0:T(2,128)(2,1)S(1)} slice(bf16[1,3,128,4096]{3,2,1,0:T(8,128)(2,1)} %inputs.1), slice={[0:1], [0:3], [126:128], [0:4096]} | slice | bytes 98304 | tf_op jit(solution)/shard_map/slice | solution.py:205
  1.0 1.7 %collective-permute-start = (bf16[1,3,2,4096]{3,2,1,0:T(2,128)(2,1)S(1)}, bf16[1,3,2,4096]{3,2,1,0:T(2,128)(2,1)S(1)}, u32[]{:S(2)}, u32[]{:S(2)}) collective-permute-start(bf16[1,3,2,4096]{3,2,1,0:T(2,128)(2,1)S(1)} %slice.17), channel_id=1, source_target_pairs={{0,32},{32,64},{64,96},{96,128},{128,160},{160,192},{192,224},{224... | collective-permute-start | bytes 147464 | tf_op jit(solution)/shard_map/ppermute | solution.py:161
  2.7 1.0 %copy.6.taps = f32[1,3,3,4096]{3,2,1,0:T(4,128)S(1)} copy(f32[1,3,3,4096]{3,0,2,1:T(1,128)} %param.6) | data formatting | bytes 294912 | tf_op args[1]
  3.8 0.0 collective-permute-done.rim
  3.8 0.0 copy-start
  3.8 1.9 %copy-done = bf16[1,3,128,4096]{3,2,1,0:T(8,128)(2,1)S(1)} copy-done((bf16[1,3,128,4096]{3,2,1,0:T(8,128)(2,1)S(1)}, bf16[1,3,128,4096]{3,2,1,0:T(8,128)(2,1)}, u32[]{:S(2)}) %copy-start) | copy-done | bytes 3145752
  5.7 0.9 copy-done.1
  6.6 5.3 %local_states.1 = (f32[4,16,8,128]{3,2,1,0:T(8,128)S(1)}, f32[4,16,8,128]{3,2,1,0:T(8,128)S(1)}, f32[4,128,8,128]{3,2,1,0:T(8,128)S(1)}, f32[4,128,8,128]{3,2,1,0:T(8,128)S(1)}) custom-call(bf16[1,3,128,4096]{3,2,1,0:T(8,128)(2,1)S(1)} %copy-done, bf16[1,3,2,4096]{3,2,1,0:T(2,128)(2,1)S(1)} %collective-permute-done.rim, f32[1,3,3,4096]{3,2,1,0:T(4,128)S(1)} %copy.6.taps, ...), custom_call_target="tpu_custom_call" | custom-call | tf_op jit(solution)/shard_map/local_states/pallas_call | solution.py:109
  11.9 0.0 copy-start.3
  11.9 1.3 %copy-done.3 = f32[4,128,8,128]{3,2,1,0:T(8,128)} copy-done((f32[4,128,8,128]{3,2,1,0:T(8,128)}, f32[4,128,8,128]{3,2,1,0:T(8,128)S(1)}, u32[]{:S(2)}) %copy-start.3) | copy-done | bytes 2097176
  13.3 4.8 %collective-permute-start.1 = (f32[4,8,8,128]{3,2,1,0:T(8,128)S(1)}, f32[4,8,8,128]{3,2,1,0:T(8,128)S(1)}, u32[]{:S(2)}, u32[]{:S(2)}) collective-permute-start(f32[4,8,8,128]{3,2,1,0:T(8,128)S(1)} %slice_select_fusion), channel_id=1, source_target_pairs={{0,32},{32,0},{64,96},{96,64},{128,160},{160,128},{192,224},{224,1... | collective-permute-start | bytes 393224 | tf_op jit(solution)/shard_map/ppermute | solution.py:161
  18.1 1.0 %collective-permute-done.1 = f32[4,8,8,128]{3,2,1,0:T(8,128)S(1)} collective-permute-done((f32[4,8,8,128]{3,2,1,0:T(8,128)S(1)}, f32[4,8,8,128]{3,2,1,0:T(8,128)S(1)}, u32[]{:S(2)}, u32[]{:S(2)}) %collective-permute-start.1) | collective-permute-done | bytes 131104 | tf_op jit(solution)/shard_map/ppermute | solution.py:161
  19.1 0.1 select_add_fusion
  19.1 4.5 %collective-permute-start.2 = (f32[4,8,8,128]{3,2,1,0:T(8,128)S(1)}, f32[4,8,8,128]{3,2,1,0:T(8,128)S(1)}, u32[]{:S(2)}, u32[]{:S(2)}) collective-permute-start(f32[4,8,8,128]{3,2,1,0:T(8,128)S(1)} %get-tuple-element.15), channel_id=1, source_target_pairs={{0,64},{32,96},{64,0},{96,32},{128,192},{160,224},{192,128},{224,1... | collective-permute-start | bytes 393224 | tf_op jit(solution)/shard_map/ppermute | solution.py:161
  23.6 3.8 %collective-permute-done.2 = f32[4,8,8,128]{3,2,1,0:T(8,128)S(1)} collective-permute-done((f32[4,8,8,128]{3,2,1,0:T(8,128)S(1)}, f32[4,8,8,128]{3,2,1,0:T(8,128)S(1)}, u32[]{:S(2)}, u32[]{:S(2)}) %collective-permute-start.2) | collective-permute-done | bytes 131104 | tf_op jit(solution)/shard_map/ppermute | solution.py:161
  27.5 7.3 %collective-permute-start.3 = (f32[4,8,8,128]{3,2,1,0:T(8,128)S(1)}, f32[4,8,8,128]{3,2,1,0:T(8,128)S(1)}, u32[]{:S(2)}, u32[]{:S(2)}) collective-permute-start(f32[4,8,8,128]{3,2,1,0:T(8,128)S(1)} %add_select_fusion.1), channel_id=1, source_target_pairs={{0,128},{32,160},{64,192},{96,224},{128,0},{160,32},{192,64},{224,... | collective-permute-start | bytes 393224 | tf_op jit(solution)/shard_map/ppermute | solution.py:161
  34.8 6.2 %collective-permute-done.3 = f32[4,8,8,128]{3,2,1,0:T(8,128)S(1)} collective-permute-done((f32[4,8,8,128]{3,2,1,0:T(8,128)S(1)}, f32[4,8,8,128]{3,2,1,0:T(8,128)S(1)}, u32[]{:S(2)}, u32[]{:S(2)}) %collective-permute-start.3) | collective-permute-done | bytes 131104 | tf_op jit(solution)/shard_map/ppermute | solution.py:161
  41.0 0.7 add_select_fusion
  41.7 7.2 %collective-permute-start.4 = (f32[4,8,8,128]{3,2,1,0:T(8,128)}, f32[4,8,8,128]{3,2,1,0:T(8,128)S(1)}, u32[]{:S(2)}, u32[]{:S(2)}) collective-permute-start(f32[4,8,8,128]{3,2,1,0:T(8,128)} %add_select_fusion), channel_id=1, source_target_pairs={{0,448},{32,480},{64,384},{96,416},{128,320},{160,352},{192,256},{... | collective-permute-start | bytes 393224 | tf_op jit(solution)/shard_map/ppermute | solution.py:161
  48.9 0.0 copy-start.4
  48.9 4.9 %collective-permute-done.4 = f32[4,8,8,128]{3,2,1,0:T(8,128)S(1)} collective-permute-done((f32[4,8,8,128]{3,2,1,0:T(8,128)}, f32[4,8,8,128]{3,2,1,0:T(8,128)S(1)}, u32[]{:S(2)}, u32[]{:S(2)}) %collective-permute-start.4) | collective-permute-done | bytes 131104 | tf_op jit(solution)/shard_map/ppermute | solution.py:161
  53.9 0.1 fusion
  54.0 1.9 %collective-permute-start.5 = (f32[4,8,8,128]{3,2,1,0:T(8,128)S(1)}, f32[4,8,8,128]{3,2,1,0:T(8,128)S(1)}, u32[]{:S(2)}, u32[]{:S(2)}) collective-permute-start(f32[4,8,8,128]{3,2,1,0:T(8,128)S(1)} %fusion), channel_id=1, source_target_pairs={{0,32},{32,0},{64,96},{96,64},{128,160},{160,128},{192,224},{224,1... | collective-permute-start | bytes 393224 | tf_op jit(solution)/shard_map/ppermute | solution.py:161
  55.9 0.0 copy-done.2
  55.9 0.0 copy-done.6
  55.9 0.2 multiply_bitcast_fusion.scaled
  56.1 1.1 %collective-permute-done.5 = f32[4,8,8,128]{3,2,1,0:T(8,128)S(1)} collective-permute-done((f32[4,8,8,128]{3,2,1,0:T(8,128)S(1)}, f32[4,8,8,128]{3,2,1,0:T(8,128)S(1)}, u32[]{:S(2)}, u32[]{:S(2)}) %collective-permute-start.5) | collective-permute-done | bytes 131104 | tf_op jit(solution)/shard_map/ppermute | solution.py:161
  57.2 0.1 broadcast_select_fusion.1
  57.4 7.0 %mixed_output.1 = bf16[1,128,4096]{2,1,0:T(8,128)(2,1)S(1)} custom-call(f32[4,128,8,128]{3,2,1,0:T(8,128)S(1)} %get-tuple-element.9.lead, f32[4,128,8,128]{3,2,1,0:T(8,128)S(1)} %copy-done.4, f32[1,16,4096]{2,1,0:T(8,128)S(1)} %copy-done.2, f32[16,4096]{1,0:T(8,128)S(1)} %multiply_bitcast_fusion.scaled, f32[1,4096]{1,0:T(1,128)S(1)} %copy-done.5, ...), custom_call_target="tpu_custom_call" | custom-call | tf_op jit(solution)/shard_map/mixed_output/pallas_call | solution.py:136
  64.4 3.4 %collective-permute-start.6 = (bf16[1,128,4096]{2,1,0:T(8,128)(2,1)S(1)}, bf16[1,128,4096]{2,1,0:T(8,128)(2,1)S(1)}, u32[]{:S(2)}, u32[]{:S(2)}) collective-permute-start(bf16[1,128,4096]{2,1,0:T(8,128)(2,1)S(1)} %mixed_output.1), channel_id=1, source_target_pairs={{0,1},{1,2},{2,3},{3,4},{4,5},{5,6},{6,7},{7,8},{8,9},{9,10},{10,1... | collective-permute-start | bytes 3145736 | tf_op jit(solution)/shard_map/ppermute | solution.py:212
  67.9 27.0 %collective-permute-done.6 = bf16[1,128,4096]{2,1,0:T(8,128)(2,1)S(1)} collective-permute-done((bf16[1,128,4096]{2,1,0:T(8,128)(2,1)S(1)}, bf16[1,128,4096]{2,1,0:T(8,128)(2,1)S(1)}, u32[]{:S(2)}, u32[]{:S(2)}) %collective-permute-start.6) | collective-permute-done | bytes 1048608 | tf_op jit(solution)/shard_map/ppermute | solution.py:212
  94.9 1.0 %copy.8 = bf16[1,128,4096]{2,1,0:T(8,128)(2,1)} copy(bf16[1,128,4096]{2,1,0:T(8,128)(2,1)S(1)} %collective-permute-done.6) | data formatting | bytes 2097152
  (10 shorter events, 0.1 us)
Async XLA Ops:
  1.0 2.8 %collective-permute-start = (bf16[1,3,2,4096]{3,2,1,0:T(2,128)(2,1)S(1)}, bf16[1,3,2,4096]{3,2,1,0:T(2,128)(2,1)S(1)}, u32[]{:S(2)}, u32[]{:S(2)}) collective-permute-start(bf16[1,3,2,4096]{3,2,1,0:T(2,128)(2,1)S(1)} %slice.17), channel_id=1, source_target_pairs={{0,32},{32,64},{64,96},{96,128},{128,160},{160,192},{192,224},{224... | collective-permute-start | bytes 147464 | tf_op jit(solution)/shard_map/ppermute | solution.py:161
  3.8 1.9 %copy-start = (bf16[1,3,128,4096]{3,2,1,0:T(8,128)(2,1)S(1)}, bf16[1,3,128,4096]{3,2,1,0:T(8,128)(2,1)}, u32[]{:S(2)}) copy-start(bf16[1,3,128,4096]{3,2,1,0:T(8,128)(2,1)} %inputs.1) | copy-start | bytes 9437188
  5.7 0.9 copy-start.1
  11.9 1.3 %copy-start.3 = (f32[4,128,8,128]{3,2,1,0:T(8,128)}, f32[4,128,8,128]{3,2,1,0:T(8,128)S(1)}, u32[]{:S(2)}) copy-start(f32[4,128,8,128]{3,2,1,0:T(8,128)S(1)} %get-tuple-element.10.gate) | copy-start | bytes 6291460
  13.3 42.6 %copy-start.2 = (f32[1,16,4096]{2,1,0:T(8,128)S(1)}, f32[1,16,4096]{2,1,0:T(8,128)}, u32[]{:S(2)}) copy-start(f32[1,16,4096]{2,1,0:T(8,128)} %rates.3) | copy-start | bytes 786436
  13.3 42.7 %copy-start.6 = (f32[1,16,4096]{2,1,0:T(8,128)S(1)}, f32[1,16,4096]{2,1,0:T(8,128)}, u32[]{:S(2)}) copy-start(f32[1,16,4096]{2,1,0:T(8,128)} %param.8) | copy-start | bytes 786436
  13.3 5.8 %collective-permute-start.1 = (f32[4,8,8,128]{3,2,1,0:T(8,128)S(1)}, f32[4,8,8,128]{3,2,1,0:T(8,128)S(1)}, u32[]{:S(2)}, u32[]{:S(2)}) collective-permute-start(f32[4,8,8,128]{3,2,1,0:T(8,128)S(1)} %slice_select_fusion), channel_id=1, source_target_pairs={{0,32},{32,0},{64,96},{96,64},{128,160},{160,128},{192,224},{224,1... | collective-permute-start | bytes 393224 | tf_op jit(solution)/shard_map/ppermute | solution.py:161
  19.1 8.3 %collective-permute-start.2 = (f32[4,8,8,128]{3,2,1,0:T(8,128)S(1)}, f32[4,8,8,128]{3,2,1,0:T(8,128)S(1)}, u32[]{:S(2)}, u32[]{:S(2)}) collective-permute-start(f32[4,8,8,128]{3,2,1,0:T(8,128)S(1)} %get-tuple-element.15), channel_id=1, source_target_pairs={{0,64},{32,96},{64,0},{96,32},{128,192},{160,224},{192,128},{224,1... | collective-permute-start | bytes 393224 | tf_op jit(solution)/shard_map/ppermute | solution.py:161
  27.5 13.5 %collective-permute-start.3 = (f32[4,8,8,128]{3,2,1,0:T(8,128)S(1)}, f32[4,8,8,128]{3,2,1,0:T(8,128)S(1)}, u32[]{:S(2)}, u32[]{:S(2)}) collective-permute-start(f32[4,8,8,128]{3,2,1,0:T(8,128)S(1)} %add_select_fusion.1), channel_id=1, source_target_pairs={{0,128},{32,160},{64,192},{96,224},{128,0},{160,32},{192,64},{224,... | collective-permute-start | bytes 393224 | tf_op jit(solution)/shard_map/ppermute | solution.py:161
  41.7 15.7 %copy-start.5 = (f32[1,4096]{1,0:T(1,128)S(1)}, f32[1,4096]{1,0:T(1,128)}, u32[]{:S(2)}) copy-start(f32[1,4096]{1,0:T(1,128)} %skip.1) | copy-start | bytes 49156
  41.7 12.2 %collective-permute-start.4 = (f32[4,8,8,128]{3,2,1,0:T(8,128)}, f32[4,8,8,128]{3,2,1,0:T(8,128)S(1)}, u32[]{:S(2)}, u32[]{:S(2)}) collective-permute-start(f32[4,8,8,128]{3,2,1,0:T(8,128)} %add_select_fusion), channel_id=1, source_target_pairs={{0,448},{32,480},{64,384},{96,416},{128,320},{160,352},{192,256},{... | collective-permute-start | bytes 393224 | tf_op jit(solution)/shard_map/ppermute | solution.py:161
  48.9 8.5 %copy-start.4 = (f32[4,128,8,128]{3,2,1,0:T(8,128)S(1)}, f32[4,128,8,128]{3,2,1,0:T(8,128)}, u32[]{:S(2)}) copy-start(f32[4,128,8,128]{3,2,1,0:T(8,128)} %copy-done.3) | copy-start | bytes 6291460
  54.0 3.2 %collective-permute-start.5 = (f32[4,8,8,128]{3,2,1,0:T(8,128)S(1)}, f32[4,8,8,128]{3,2,1,0:T(8,128)S(1)}, u32[]{:S(2)}, u32[]{:S(2)}) collective-permute-start(f32[4,8,8,128]{3,2,1,0:T(8,128)S(1)} %fusion), channel_id=1, source_target_pairs={{0,32},{32,0},{64,96},{96,64},{128,160},{160,128},{192,224},{224,1... | collective-permute-start | bytes 393224 | tf_op jit(solution)/shard_map/ppermute | solution.py:161
  64.4 30.4 %collective-permute-start.6 = (bf16[1,128,4096]{2,1,0:T(8,128)(2,1)S(1)}, bf16[1,128,4096]{2,1,0:T(8,128)(2,1)S(1)}, u32[]{:S(2)}, u32[]{:S(2)}) collective-permute-start(bf16[1,128,4096]{2,1,0:T(8,128)(2,1)S(1)} %mixed_output.1), channel_id=1, source_target_pairs={{0,1},{1,2},{2,3},{3,4},{4,5},{5,6},{6,7},{7,8},{8,9},{9,10},{10,1... | collective-permute-start | bytes 3145736 | tf_op jit(solution)/shard_map/ppermute | solution.py:212

commit v2 on v1

--- a/solution.py
+++ b/solution.py
@@ -161,6 +161,10 @@
     return lax.ppermute(x, "seq", pairs)
 
 
+def carried(x, pairs):
+    return moved(x.astype(jnp.bfloat16), pairs).astype(jnp.float32)
+
+
 def prefix(ends, span):
     nseq = lax.axis_size("seq")
     chips = nseq // 2
@@ -173,7 +177,7 @@
     mine = lambda x: jnp.where(first, low(x), high(x))
     others = lambda x: jnp.where(first, high(x), low(x))
     swap = [(i, i ^ 1) for i in range(nseq)]
-    own, came = mine(ends), moved(others(ends), swap)
+    own, came = mine(ends), carried(others(ends), swap)
     span = mine(span)
     zeroth, oneth = jnp.where(first, own, came), jnp.where(first, came, own)
     fade = jnp.exp(-span)
@@ -181,7 +185,7 @@
     enter = None
     step = 1
     while step < chips // 2:
-        came = moved(whole, [(i, ((i // 2) ^ step) * 2 + i % 2) for i in range(nseq)])
+        came = carried(whole, [(i, ((i // 2) ^ step) * 2 + i % 2) for i in range(nseq)])
         right = (chip & step) != 0
         far = jnp.exp(-span * (2 * (chip & (step - 1))).astype(jnp.float32))
         into = jnp.where(right, far * came, 0.0)
@@ -189,11 +193,11 @@
         fading = jnp.exp(-span * (2.0 * step))
         whole = jnp.where(right, fading * came + whole, fading * whole + came)
         step *= 2
-    came = moved(whole, [(c * 2 + k, (chips - 1 - c) * 2 + k) for c in range(chips // 2) for k in range(2)])
+    came = carried(whole, [(c * 2 + k, (chips - 1 - c) * 2 + k) for c in range(chips // 2) for k in range(2)])
     far = jnp.exp(-span * (2 * (chip & (step - 1))).astype(jnp.float32))
     enter = enter + far * came
     second = fade * enter + zeroth
-    came = moved(jnp.where(first, second, enter), swap)
+    came = carried(jnp.where(first, second, enter), swap)
     own = jnp.where(first, enter, second)
     return jnp.concatenate([jnp.where(first, own, came), jnp.where(first, came, own)], axis=1)
 

time: 96.3 us -> 89.1 us (0.925)
  waiting for transfers between devices: 44.1 us -> 37.4 us
    ppermute x6, waiting for transfers between devices: 17 us -> 10.4 us  [moved(): return lax.ppermute(x, 'seq', pairs)]
where the time goes in v2:
time: 89.1 us; the launch traced here: 88.7 us
  waiting for transfers between devices  37.4 us (42%)
  starting transfers between devices  30.9 us (35%)
  Pallas kernels  12.3 us (14%)
  local copies, waits for them, and re-layouts  7.14 us (8%)
    ppermute x6, starting transfers between devices, moved(): return lax.ppermute(x, 'seq', pairs)  27.5 us
    ppermute x1, waiting for transfers between devices, shards(): lax.ppermute(output, 'pipe', [(i, i + 1) for i in range(sections - 1)])  27 us
    ppermute x6, waiting for transfers between devices, moved(): return lax.ppermute(x, 'seq', pairs)  10.4 us
    pallas_call x1, Pallas kernels, mixed_output(): pl.pallas_call(functools.partial(output_kernel, order, length, pitch, tot...  7.03 us
    unnamed x16, local copies, waits for them, and re-layouts  6.16 us
    pallas_call x1, Pallas kernels, local_states(): pl.pallas_call(functools.partial(state_kernel, order, length, pitch, tota...  5.3 us
    ppermute x1, starting transfers between devices, shards(): lax.ppermute(output, 'pipe', [(i, i + 1) for i in range(sections - 1)])  3.4 us
  transfers between devices with their start and end apart: 7, of which 6 were waited for; matrix products, arithmetic and copies ran while one was open for 1% of the time, Pallas kernels for 0%

profile of v2, /device:TPU:32, one launch (start us, length us, event | category | flops | bytes accessed | tf_op | source)
XLA Modules:
  0.0 88.7 jit_solution(166563762265258456)
XLA Ops:
  0.0 1.0 %slice.17 = bf16[1,3,2,4096]{3,2,1,0:T(2,128)(2,1)S(1)} slice(bf16[1,3,128,4096]{3,2,1,0:T(8,128)(2,1)} %inputs.1), slice={[0:1], [0:3], [126:128], [0:4096]} | slice | bytes 98304 | tf_op jit(solution)/shard_map/slice | solution.py:209
  1.0 1.7 %collective-permute-start = (bf16[1,3,2,4096]{3,2,1,0:T(2,128)(2,1)S(1)}, bf16[1,3,2,4096]{3,2,1,0:T(2,128)(2,1)S(1)}, u32[]{:S(2)}, u32[]{:S(2)}) collective-permute-start(bf16[1,3,2,4096]{3,2,1,0:T(2,128)(2,1)S(1)} %slice.17), channel_id=1, source_target_pairs={{0,32},{32,64},{64,96},{96,128},{128,160},{160,192},{192,224},{224... | collective-permute-start | bytes 147464 | tf_op jit(solution)/shard_map/ppermute | solution.py:161
  2.7 1.0 %copy.6.taps = f32[1,3,3,4096]{3,2,1,0:T(4,128)S(1)} copy(f32[1,3,3,4096]{3,0,2,1:T(1,128)} %param.6) | data formatting | bytes 294912 | tf_op args[1]
  3.8 0.0 collective-permute-done.rim
  3.8 0.0 copy-start
  3.8 1.9 %copy-done = bf16[1,3,128,4096]{3,2,1,0:T(8,128)(2,1)S(1)} copy-done((bf16[1,3,128,4096]{3,2,1,0:T(8,128)(2,1)S(1)}, bf16[1,3,128,4096]{3,2,1,0:T(8,128)(2,1)}, u32[]{:S(2)}) %copy-start) | copy-done | bytes 3145752
  5.7 0.9 %copy-done.1 = f32[1,16,4096]{2,1,0:T(8,128)S(1)} copy-done((f32[1,16,4096]{2,1,0:T(8,128)S(1)}, f32[1,16,4096]{2,1,0:T(8,128)}, u32[]{:S(2)}) %copy-start.1) | copy-done | bytes 262168
  6.6 5.3 %local_states.1 = (f32[4,16,8,128]{3,2,1,0:T(8,128)S(1)}, f32[4,16,8,128]{3,2,1,0:T(8,128)S(1)}, f32[4,128,8,128]{3,2,1,0:T(8,128)S(1)}, f32[4,128,8,128]{3,2,1,0:T(8,128)S(1)}) custom-call(bf16[1,3,128,4096]{3,2,1,0:T(8,128)(2,1)S(1)} %copy-done, bf16[1,3,2,4096]{3,2,1,0:T(2,128)(2,1)S(1)} %collective-permute-done.rim, f32[1,3,3,4096]{3,2,1,0:T(4,128)S(1)} %copy.6.taps, ...), custom_call_target="tpu_custom_call" | custom-call | tf_op jit(solution)/shard_map/local_states/pallas_call | solution.py:109
  11.9 1.3 %copy-done.3 = f32[4,128,8,128]{3,2,1,0:T(8,128)} copy-done((f32[4,128,8,128]{3,2,1,0:T(8,128)}, f32[4,128,8,128]{3,2,1,0:T(8,128)S(1)}, u32[]{:S(2)}) %copy-start.3) | copy-done | bytes 2097176
  13.3 4.8 %collective-permute-start.1 = (bf16[4,8,8,128]{3,2,1,0:T(8,128)(2,1)S(1)}, bf16[4,8,8,128]{3,2,1,0:T(8,128)(2,1)S(1)}, u32[]{:S(2)}, u32[]{:S(2)}) collective-permute-start(bf16[4,8,8,128]{3,2,1,0:T(8,128)(2,1)S(1)} %select_convert_fusion.1), channel_id=1, source_target_pairs={{0,32},{32,0},{64,96},{96,64},{128,160},{160,128},{192,224},{224,1... | collective-permute-start | bytes 196616 | tf_op jit(solution)/shard_map/ppermute | solution.py:161
  18.1 0.9 collective-permute-done.1
  19.0 0.1 fusion.11
  19.0 0.0 copy-start.5
  19.0 4.5 %collective-permute-start.2 = (bf16[4,8,8,128]{3,2,1,0:T(8,128)(2,1)S(1)}, bf16[4,8,8,128]{3,2,1,0:T(8,128)(2,1)S(1)}, u32[]{:S(2)}, u32[]{:S(2)}) collective-permute-start(bf16[4,8,8,128]{3,2,1,0:T(8,128)(2,1)S(1)} %get-tuple-element.15), channel_id=1, source_target_pairs={{0,64},{32,96},{64,0},{96,32},{128,192},{160,224},{192,128},{224,1... | collective-permute-start | bytes 196616 | tf_op jit(solution)/shard_map/ppermute | solution.py:161
  23.6 2.4 %collective-permute-done.2 = bf16[4,8,8,128]{3,2,1,0:T(8,128)(2,1)S(1)} collective-permute-done((bf16[4,8,8,128]{3,2,1,0:T(8,128)(2,1)S(1)}, bf16[4,8,8,128]{3,2,1,0:T(8,128)(2,1)S(1)}, u32[]{:S(2)}, u32[]{:S(2)}) %collective-permute-start.2) | collective-permute-done | bytes 65568 | tf_op jit(solution)/shard_map/ppermute | solution.py:161
  25.9 0.1 fusion.12
  26.0 7.3 %collective-permute-start.3 = (bf16[4,8,8,128]{3,2,1,0:T(8,128)(2,1)S(1)}, bf16[4,8,8,128]{3,2,1,0:T(8,128)(2,1)S(1)}, u32[]{:S(2)}, u32[]{:S(2)}) collective-permute-start(bf16[4,8,8,128]{3,2,1,0:T(8,128)(2,1)S(1)} %fusion.12), channel_id=1, source_target_pairs={{0,128},{32,160},{64,192},{96,224},{128,0},{160,32},{192,64},{224,... | collective-permute-start | bytes 196616 | tf_op jit(solution)/shard_map/ppermute | solution.py:161
  33.3 3.6 %collective-permute-done.3 = bf16[4,8,8,128]{3,2,1,0:T(8,128)(2,1)S(1)} collective-permute-done((bf16[4,8,8,128]{3,2,1,0:T(8,128)(2,1)S(1)}, bf16[4,8,8,128]{3,2,1,0:T(8,128)(2,1)S(1)}, u32[]{:S(2)}, u32[]{:S(2)}) %collective-permute-start.3) | collective-permute-done | bytes 65568 | tf_op jit(solution)/shard_map/ppermute | solution.py:161
  37.0 0.1 fusion.9
  37.1 7.2 %collective-permute-start.4 = (bf16[4,8,8,128]{3,2,1,0:T(8,128)(2,1)S(1)}, bf16[4,8,8,128]{3,2,1,0:T(8,128)(2,1)S(1)}, u32[]{:S(2)}, u32[]{:S(2)}) collective-permute-start(bf16[4,8,8,128]{3,2,1,0:T(8,128)(2,1)S(1)} %fusion.9), channel_id=1, source_target_pairs={{0,448},{32,480},{64,384},{96,416},{128,320},{160,352},{192,256},{... | collective-permute-start | bytes 196616 | tf_op jit(solution)/shard_map/ppermute | solution.py:161
  44.3 2.5 %collective-permute-done.4 = bf16[4,8,8,128]{3,2,1,0:T(8,128)(2,1)S(1)} collective-permute-done((bf16[4,8,8,128]{3,2,1,0:T(8,128)(2,1)S(1)}, bf16[4,8,8,128]{3,2,1,0:T(8,128)(2,1)S(1)}, u32[]{:S(2)}, u32[]{:S(2)}) %collective-permute-start.4) | collective-permute-done | bytes 65568 | tf_op jit(solution)/shard_map/ppermute | solution.py:161
  46.8 0.1 select_convert_fusion
  46.9 1.9 %collective-permute-start.5 = (bf16[4,8,8,128]{3,2,1,0:T(8,128)(2,1)S(1)}, bf16[4,8,8,128]{3,2,1,0:T(8,128)(2,1)S(1)}, u32[]{:S(2)}, u32[]{:S(2)}) collective-permute-start(bf16[4,8,8,128]{3,2,1,0:T(8,128)(2,1)S(1)} %select_convert_fusion), channel_id=1, source_target_pairs={{0,32},{32,0},{64,96},{96,64},{128,160},{160,128},{192,224},{224,1... | collective-permute-start | bytes 196616 | tf_op jit(solution)/shard_map/ppermute | solution.py:161
  48.9 0.2 multiply_bitcast_fusion.scaled
  49.1 1.0 %collective-permute-done.5 = bf16[4,8,8,128]{3,2,1,0:T(8,128)(2,1)S(1)} collective-permute-done((bf16[4,8,8,128]{3,2,1,0:T(8,128)(2,1)S(1)}, bf16[4,8,8,128]{3,2,1,0:T(8,128)(2,1)S(1)}, u32[]{:S(2)}, u32[]{:S(2)}) %collective-permute-start.5) | collective-permute-done | bytes 65568 | tf_op jit(solution)/shard_map/ppermute | solution.py:161
  50.1 0.1 convert_select_fusion.1
  50.3 0.0 copy-done.5
  50.3 0.0 copy-done.4
  50.3 7.0 %mixed_output.1 = bf16[1,128,4096]{2,1,0:T(8,128)(2,1)S(1)} custom-call(f32[4,128,8,128]{3,2,1,0:T(8,128)S(1)} %get-tuple-element.9.lead, f32[4,128,8,128]{3,2,1,0:T(8,128)S(1)} %copy-done.4, f32[1,16,4096]{2,1,0:T(8,128)S(1)} %copy-done.2, f32[16,4096]{1,0:T(8,128)S(1)} %multiply_bitcast_fusion.scaled, f32[1,4096]{1,0:T(1,128)S(1)} %copy-done.5, ...), custom_call_target="tpu_custom_call" | custom-call | tf_op jit(solution)/shard_map/mixed_output/pallas_call | solution.py:136
  57.3 3.4 %collective-permute-start.6 = (bf16[1,128,4096]{2,1,0:T(8,128)(2,1)S(1)}, bf16[1,128,4096]{2,1,0:T(8,128)(2,1)S(1)}, u32[]{:S(2)}, u32[]{:S(2)}) collective-permute-start(bf16[1,128,4096]{2,1,0:T(8,128)(2,1)S(1)} %mixed_output.1), channel_id=1, source_target_pairs={{0,1},{1,2},{2,3},{3,4},{4,5},{5,6},{6,7},{7,8},{8,9},{9,10},{10,1... | collective-permute-start | bytes 3145736 | tf_op jit(solution)/shard_map/ppermute | solution.py:216
  60.7 27.0 %collective-permute-done.6 = bf16[1,128,4096]{2,1,0:T(8,128)(2,1)S(1)} collective-permute-done((bf16[1,128,4096]{2,1,0:T(8,128)(2,1)S(1)}, bf16[1,128,4096]{2,1,0:T(8,128)(2,1)S(1)}, u32[]{:S(2)}, u32[]{:S(2)}) %collective-permute-start.6) | collective-permute-done | bytes 1048608 | tf_op jit(solution)/shard_map/ppermute | solution.py:216
  87.8 1.0 %copy.8 = bf16[1,128,4096]{2,1,0:T(8,128)(2,1)} copy(bf16[1,128,4096]{2,1,0:T(8,128)(2,1)S(1)} %collective-permute-done.6) | data formatting | bytes 2097152
  (10 shorter events, 0.1 us)
Async XLA Ops:
  1.0 2.8 %collective-permute-start = (bf16[1,3,2,4096]{3,2,1,0:T(2,128)(2,1)S(1)}, bf16[1,3,2,4096]{3,2,1,0:T(2,128)(2,1)S(1)}, u32[]{:S(2)}, u32[]{:S(2)}) collective-permute-start(bf16[1,3,2,4096]{3,2,1,0:T(2,128)(2,1)S(1)} %slice.17), channel_id=1, source_target_pairs={{0,32},{32,64},{64,96},{96,128},{128,160},{160,192},{192,224},{224... | collective-permute-start | bytes 147464 | tf_op jit(solution)/shard_map/ppermute | solution.py:161
  3.8 1.9 %copy-start = (bf16[1,3,128,4096]{3,2,1,0:T(8,128)(2,1)S(1)}, bf16[1,3,128,4096]{3,2,1,0:T(8,128)(2,1)}, u32[]{:S(2)}) copy-start(bf16[1,3,128,4096]{3,2,1,0:T(8,128)(2,1)} %inputs.1) | copy-start | bytes 9437188
  5.7 0.9 %copy-start.1 = (f32[1,16,4096]{2,1,0:T(8,128)S(1)}, f32[1,16,4096]{2,1,0:T(8,128)}, u32[]{:S(2)}) copy-start(f32[1,16,4096]{2,1,0:T(8,128)} %rates.3) | copy-start | bytes 786436
  11.9 1.3 %copy-start.3 = (f32[4,128,8,128]{3,2,1,0:T(8,128)}, f32[4,128,8,128]{3,2,1,0:T(8,128)S(1)}, u32[]{:S(2)}) copy-start(f32[4,128,8,128]{3,2,1,0:T(8,128)S(1)} %get-tuple-element.10.gate) | copy-start | bytes 6291460
  13.3 35.6 %copy-start.2 = (f32[1,16,4096]{2,1,0:T(8,128)S(1)}, f32[1,16,4096]{2,1,0:T(8,128)}, u32[]{:S(2)}) copy-start(f32[1,16,4096]{2,1,0:T(8,128)} %rates.3) | copy-start | bytes 786436
  13.3 35.6 %copy-start.6 = (f32[1,16,4096]{2,1,0:T(8,128)S(1)}, f32[1,16,4096]{2,1,0:T(8,128)}, u32[]{:S(2)}) copy-start(f32[1,16,4096]{2,1,0:T(8,128)} %param.8) | copy-start | bytes 786436
  13.3 5.7 %collective-permute-start.1 = (bf16[4,8,8,128]{3,2,1,0:T(8,128)(2,1)S(1)}, bf16[4,8,8,128]{3,2,1,0:T(8,128)(2,1)S(1)}, u32[]{:S(2)}, u32[]{:S(2)}) collective-permute-start(bf16[4,8,8,128]{3,2,1,0:T(8,128)(2,1)S(1)} %select_convert_fusion.1), channel_id=1, source_target_pairs={{0,32},{32,0},{64,96},{96,64},{128,160},{160,128},{192,224},{224,1... | collective-permute-start | bytes 196616 | tf_op jit(solution)/shard_map/ppermute | solution.py:161
  19.0 31.2 %copy-start.5 = (f32[1,4096]{1,0:T(1,128)S(1)}, f32[1,4096]{1,0:T(1,128)}, u32[]{:S(2)}) copy-start(f32[1,4096]{1,0:T(1,128)} %skip.1) | copy-start | bytes 49156
  19.0 6.9 %collective-permute-start.2 = (bf16[4,8,8,128]{3,2,1,0:T(8,128)(2,1)S(1)}, bf16[4,8,8,128]{3,2,1,0:T(8,128)(2,1)S(1)}, u32[]{:S(2)}, u32[]{:S(2)}) collective-permute-start(bf16[4,8,8,128]{3,2,1,0:T(8,128)(2,1)S(1)} %get-tuple-element.15), channel_id=1, source_target_pairs={{0,64},{32,96},{64,0},{96,32},{128,192},{160,224},{192,128},{224,1... | collective-permute-start | bytes 196616 | tf_op jit(solution)/shard_map/ppermute | solution.py:161
  26.0 10.9 %collective-permute-start.3 = (bf16[4,8,8,128]{3,2,1,0:T(8,128)(2,1)S(1)}, bf16[4,8,8,128]{3,2,1,0:T(8,128)(2,1)S(1)}, u32[]{:S(2)}, u32[]{:S(2)}) collective-permute-start(bf16[4,8,8,128]{3,2,1,0:T(8,128)(2,1)S(1)} %fusion.12), channel_id=1, source_target_pairs={{0,128},{32,160},{64,192},{96,224},{128,0},{160,32},{192,64},{224,... | collective-permute-start | bytes 196616 | tf_op jit(solution)/shard_map/ppermute | solution.py:161
  37.1 9.7 %collective-permute-start.4 = (bf16[4,8,8,128]{3,2,1,0:T(8,128)(2,1)S(1)}, bf16[4,8,8,128]{3,2,1,0:T(8,128)(2,1)S(1)}, u32[]{:S(2)}, u32[]{:S(2)}) collective-permute-start(bf16[4,8,8,128]{3,2,1,0:T(8,128)(2,1)S(1)} %fusion.9), channel_id=1, source_target_pairs={{0,448},{32,480},{64,384},{96,416},{128,320},{160,352},{192,256},{... | collective-permute-start | bytes 196616 | tf_op jit(solution)/shard_map/ppermute | solution.py:161
  44.3 6.0 %copy-start.4 = (f32[4,128,8,128]{3,2,1,0:T(8,128)S(1)}, f32[4,128,8,128]{3,2,1,0:T(8,128)}, u32[]{:S(2)}) copy-start(f32[4,128,8,128]{3,2,1,0:T(8,128)} %copy-done.3) | copy-start | bytes 6291460
  46.9 3.1 %collective-permute-start.5 = (bf16[4,8,8,128]{3,2,1,0:T(8,128)(2,1)S(1)}, bf16[4,8,8,128]{3,2,1,0:T(8,128)(2,1)S(1)}, u32[]{:S(2)}, u32[]{:S(2)}) collective-permute-start(bf16[4,8,8,128]{3,2,1,0:T(8,128)(2,1)S(1)} %select_convert_fusion), channel_id=1, source_target_pairs={{0,32},{32,0},{64,96},{96,64},{128,160},{160,128},{192,224},{224,1... | collective-permute-start | bytes 196616 | tf_op jit(solution)/shard_map/ppermute | solution.py:161
  57.3 30.4 %collective-permute-start.6 = (bf16[1,128,4096]{2,1,0:T(8,128)(2,1)S(1)}, bf16[1,128,4096]{2,1,0:T(8,128)(2,1)S(1)}, u32[]{:S(2)}, u32[]{:S(2)}) collective-permute-start(bf16[1,128,4096]{2,1,0:T(8,128)(2,1)S(1)} %mixed_output.1), channel_id=1, source_target_pairs={{0,1},{1,2},{2,3},{3,4},{4,5},{5,6},{6,7},{7,8},{8,9},{9,10},{10,1... | collective-permute-start | bytes 3145736 | tf_op jit(solution)/shard_map/ppermute | solution.py:216

commit v3 on v0

v3 whole, which is shorter than its diff:
```python
import functools

import jax
import jax.numpy as jnp
from jax import lax
from jax.experimental import pallas as pl
from jax.experimental.pallas import tpu as pltpu
from jax.sharding import PartitionSpec as P

TAPS = 3
LANES = 128
ROWS = 8
GROUP = ROWS * LANES
PARTS = 2
PLACE_OPS = 10000
f32 = jnp.float32
bf16 = jnp.bfloat16


def tree_sum(parts):
    while len(parts) > 1:
        parts = [parts[i] + parts[i + 1] for i in range(0, len(parts), 2)]
    return parts[0]


def by_mode(rows, values, order):
    for k in range(ROWS):
        rows[pl.ds(k * order, order), :] = values[:, k * LANES : (k + 1) * LANES]
    return [rows[pl.ds(n, ROWS, stride=order), :] for n in range(order)]


def state_kernel(order, length, pitch, total,
                 inputs, tap_source, rate_source, end_ref, span_ref, head, gate,
                 held_inputs, taps, rates, raw, mode_rows, sems):
    groups = held_inputs.shape[0]

    def fetch(g):
        return pltpu.make_async_copy(
            inputs.at[0, pl.ds(1, 2), :, pl.ds(g * GROUP, GROUP)], held_inputs.at[g], sems.at[g]
        )

    tap_copy = pltpu.make_async_copy(tap_source, taps, sems.at[groups])
    rate_copy = pltpu.make_async_copy(rate_source.at[0], rates, sems.at[groups + 1])
    fetch(0).start()
    tap_copy.start()
    rate_copy.start()
    for g in range(1, groups):
        fetch(g).start()
    zero = jnp.zeros((ROWS, LANES), f32)

    for g in range(groups):
        at = pl.ds(g * ROWS, ROWS)
        fetch(g).wait()
        for i in range(2):
            for k in range(ROWS):
                raw[i, pl.ds(k * pitch + 8, length), :] = held_inputs[g, i, :, k * LANES : (k + 1) * LANES].astype(f32)
        if g == 0:
            tap_copy.wait()
            rate_copy.wait()

        def token(i, t):
            return raw[i, pl.ds(8 + t, ROWS, stride=pitch), :]

        weights = [[taps[TAPS * (1 + i) + a, at, :] for a in range(TAPS)] for i in range(2)]

        def features(t, before):
            after, made = [], []
            for i in range(2):
                now = token(i, t)
                one, two = before[i]
                made.append(weights[i][0] * now + weights[i][1] * one + weights[i][2] * two)
                after.append((now, one))
            return tuple(after), made

        def feature_step(pair, before):
            gates = []
            for sub in range(2):
                before, made = features(2 * pair + sub, before)
                gates.append(made[0] * made[1])
            gate[g, pair] = jnp.concatenate(gates, axis=0).astype(bf16)
            return before

        before = ((zero, zero),) * 2
        for t in range(TAPS - 1):
            before, made = features(t, before)
            for i in range(2):
                head[2 * i + t, at, :] = made[i]
        lax.fori_loop(1, length // 2, feature_step, before, unroll=9)

        steps = []
        for n, rate in enumerate(by_mode(mode_rows, rates[:, g * GROUP : (g + 1) * GROUP], order)):
            span_ref[n, at, :] = rate * (length / total)
            steps.append(jnp.exp(-(rate / total)))

        def state_step(pair, states):
            both = gate[g, pair].astype(f32)
            for sub in range(2):
                gated = both[sub * ROWS : (sub + 1) * ROWS]
                states = tuple(s * x + gated for s, x in zip(steps, states))
            return states

        states = lax.fori_loop(1, length // 2, state_step, (zero,) * order, unroll=3)
        for n in range(order):
            end_ref[n, at, :] = states[n]


def patch_kernel(order, length, rim, head, taps, ends, span, wire, edge, rows):
    tiles = ends.shape[1]
    for i in range(3):
        came = rim[0, i].astype(f32)
        for t in range(TAPS - 1):
            for k in range(tiles):
                rows[2 * i + t, pl.ds(k, 1), :] = came[t : t + 1, k * LANES : (k + 1) * LANES]
    edge[0] = rows[0]
    edge[1] = rows[1]
    made = []
    for i in range(1, 3):
        two, one = rows[2 * i], rows[2 * i + 1]
        made.append((head[2 * i - 2] + taps[TAPS * i + 1] * one + taps[TAPS * i + 2] * two,
                     head[2 * i - 1] + taps[TAPS * i + 2] * one))
    gated = []
    for t in range(2):
        gated.append((made[0][t] * made[1][t]).astype(bf16).astype(f32))
        edge[2 + t] = gated[t]
    for n in range(order):
        step = span[n] * (1.0 / length)
        first = jnp.exp(-step) * gated[0] + gated[1]
        wire[n] = (ends[n] + jnp.exp(-(length - 2) * step) * first).astype(bf16)


def mix_kernel(order, length, pitch, total, inputs, taps, gate, edge, rates, scaled, skip, lead, mix, raw, mode_rows):
    steps = [jnp.exp(-(rate / total)) for rate in by_mode(mode_rows, rates[0], order)]
    scales = by_mode(mode_rows, scaled[...], order)
    weights = [taps[a] for a in range(TAPS)]
    for k in range(ROWS):
        raw[pl.ds(k * pitch, length), :] = inputs[0, 0, :, k * LANES : (k + 1) * LANES].astype(f32)

    def lead_step(pair, before):
        for sub in range(2):
            t = 2 * pair + sub
            one, two = before
            now = raw[pl.ds(t, ROWS, stride=pitch), :]
            lead[0, t] = weights[0] * now + weights[1] * one + weights[2] * two
            before = (now, one)
        return before

    lax.fori_loop(0, length // 2, lead_step, (edge[1], edge[0]), unroll=4)

    def tokens(pair, states, both):
        for sub, gated in enumerate(both):
            states = tuple(s * x + gated for s, x in zip(steps, states))
            mix[0, 2 * pair + sub] = tree_sum([w * x for w, x in zip(scales, states)]) + skip[...] * gated
        return states

    def step(pair, states):
        both = gate[0, pair].astype(f32)
        return tokens(pair, states, (both[:ROWS], both[ROWS:]))

    states = tokens(0, (jnp.zeros((ROWS, LANES), f32),) * order, (edge[2], edge[3]))
    lax.fori_loop(1, length // 2, step, states)


def finish_kernel(order, length, total, lead, mix, rates, scaled, start, out_ref, rows, mode_rows, start_rows):
    steps = [jnp.exp(-(rate / total)) for rate in by_mode(mode_rows, rates[0], order)]
    scales = by_mode(mode_rows, scaled[...], order)
    start_rows[...] = start[...].astype(f32)
    at = pl.ds(pl.multiple_of(pl.program_id(0) * ROWS, ROWS), ROWS)

    def step(t, terms):
        terms = tuple(s * x for s, x in zip(steps, terms))
        rows[pl.ds(t, ROWS, stride=length), :] = lead[0, t] * (mix[0, t] + tree_sum(list(terms)))
        return terms

    lax.fori_loop(0, length, step, tuple(scales[n] * start_rows[n, at, :] for n in range(order)), unroll=4)
    for k in range(ROWS):
        out_ref[0, :, pl.ds(k * LANES, LANES)] = rows[pl.ds(k * length, length), :].astype(bf16)


def place_kernel(part, *rest):
    rest[-1][...] = part[...]


def scan_kernel(came, span, enter):
    keep = jnp.exp(-span[lax.axis_index("seq")])
    state = jnp.zeros(keep.shape, f32)
    for j in range(came.shape[0]):
        enter[j] = state.astype(bf16)
        state = keep * state + came[j].astype(f32)


def after(*arrays):
    return lax.optimization_barrier(arrays)


def call(body, name, groups, ops, length, in_specs, out_specs, out_shape, scratch, aliases={}):
    return pl.pallas_call(
        body,
        grid=(groups,),
        in_specs=in_specs,
        out_specs=out_specs,
        out_shape=out_shape,
        scratch_shapes=scratch,
        input_output_aliases=aliases,
        compiler_params=pltpu.CompilerParams(vmem_limit_bytes=16 << 20),
        cost_estimate=pl.CostEstimate(
            flops=ops * length * groups * GROUP, bytes_accessed=8 * length * groups * GROUP, transcendentals=0
        ),
        name=name,
    )


def shards(projected, short_filter, decay_rate, residue, skip_gain):
    length, width = projected.shape[2:]
    order = decay_rate.shape[1]
    nseq = lax.axis_size("seq")
    sections = lax.axis_size("pipe")
    total = length * nseq
    groups = width // GROUP
    tiles = width // LANES
    pitch = length + 8
    onward = [(i, i + 1) for i in range(sections - 1)]
    held = lambda x: pltpu.with_memory_space_constraint(x, pltpu.HBM)
    to_all = lambda x: lax.all_to_all(x, "seq", 0, 0, tiled=True)
    taps = short_filter.reshape(3 * TAPS, tiles, LANES)
    skip = skip_gain.reshape(tiles, LANES)
    rim = lax.ppermute(projected[:, :, length - (TAPS - 1) :, :], "seq", [(i, i + 1) for i in range(nseq - 1)])

    tokens = lambda at: pl.BlockSpec((1, length, ROWS, LANES), lambda g: (at + g, 0, 0, 0))
    pairs = lambda at: pl.BlockSpec((1, length // 2, 2 * ROWS, LANES), lambda g: (at + g, 0, 0, 0))
    stack = lambda n, at: pl.BlockSpec((n, ROWS, LANES), lambda g: (0, at + g, 0))
    rate_block = lambda at: pl.BlockSpec((1, order, GROUP), lambda g: (0, 0, at + g))
    scale_block = lambda at: pl.BlockSpec((order, GROUP), lambda g: (0, at + g))
    out_block = lambda at: pl.BlockSpec((1, length, GROUP), lambda g: (0, 0, at + g))
    anywhere = pl.BlockSpec(memory_space=pl.ANY)
    shape = lambda *dims: jax.ShapeDtypeStruct(dims, f32)
    mode_rows = pltpu.VMEM((ROWS * order, LANES), f32)
    ends, span, head, gate = pl.pallas_call(
        functools.partial(state_kernel, order, length, pitch, total),
        in_specs=[anywhere] * 3,
        out_shape=[
            shape(order, tiles, LANES), shape(order, tiles, LANES), shape(4, tiles, LANES),
            jax.ShapeDtypeStruct((groups, length // 2, 2 * ROWS, LANES), bf16),
        ],
        scratch_shapes=[
            pltpu.VMEM((groups, 2, length, GROUP), bf16),
            pltpu.VMEM((3 * TAPS, tiles, LANES), f32),
            pltpu.VMEM((order, width), f32),
            pltpu.VMEM((2, ROWS * pitch, LANES), f32),
            mode_rows,
            pltpu.SemaphoreType.DMA((groups + 2,)),
        ],
        compiler_params=pltpu.CompilerParams(vmem_limit_bytes=16 << 20),
        cost_estimate=pl.CostEstimate(flops=55 * length * width, bytes_accessed=8 * length * width, transcendentals=0),
        name="local_states",
    )(held(projected), held(taps), held(decay_rate))
    wire, edge = pl.pallas_call(
        functools.partial(patch_kernel, order, length),
        out_shape=[jax.ShapeDtypeStruct((order, tiles, LANES), bf16), shape(4, tiles, LANES)],
        scratch_shapes=[pltpu.VMEM((6, tiles, LANES), f32)],
        compiler_params=pltpu.CompilerParams(vmem_limit_bytes=8 << 20),
        name="first_tokens",
    )(rim, head, taps, ends, span)

    share = groups // PARTS

    def local_mix(part, gated):
        at = part * share
        return call(
            functools.partial(mix_kernel, order, length, length, total), "local_mix", share, 80, length,
            [pl.BlockSpec((1, 1, length, GROUP), lambda g: (0, 0, 0, at + g)), stack(TAPS, at),
             pairs(at), stack(4, at), rate_block(at), scale_block(at),
             pl.BlockSpec((ROWS, LANES), lambda g: (at + g, 0))],
            [tokens(0), tokens(0)], [pltpu.HBM((share, length, ROWS, LANES), f32)] * 2,
            [pltpu.VMEM((ROWS * length, LANES), f32), mode_rows],
        )(held(projected), held(taps), gated, edge, held(decay_rate), scaled, held(skip))

    mixes = [None] * PARTS
    wire, gate, residue = after(wire, gate, residue)
    scaled = residue[0] * jnp.sqrt(-jnp.expm1(-2.0 * (decay_rate[0] / total)))
    came = to_all(wire)
    mixes[0] = local_mix(0, gate)
    came, mixes[0], gate = after(came, mixes[0], gate)
    enter = pl.pallas_call(
        scan_kernel,
        out_shape=jax.ShapeDtypeStruct(came.shape, bf16),
        compiler_params=pltpu.CompilerParams(vmem_limit_bytes=4 << 20),
        name="scan_chunks",
    )(came, span)
    enter, gate = after(enter, gate)
    start = to_all(enter)
    mixes[1] = local_mix(1, gate)
    start, mixes[1] = after(start, mixes[1])
    handed = None
    for part in range(PARTS):
        at = part * share
        output = call(
            functools.partial(finish_kernel, order, length, total), "finished", share, 40, length,
            [tokens(0), tokens(0), rate_block(at), scale_block(at),
             pl.BlockSpec((order, share * ROWS, LANES), lambda g, part=part: (0, part, 0))],
            out_block(0), jax.ShapeDtypeStruct((1, length, share * GROUP), bf16),
            [pltpu.VMEM((ROWS * length, LANES), f32), mode_rows, pltpu.VMEM((order, share * ROWS, LANES), f32)],
        )(*map(held, mixes[part]), decay_rate, scaled, start)
        came = lax.ppermute(output, "pipe", onward)
        given = [came] if handed is None else [came, handed]
        handed = call(
            place_kernel, "placed", share, PLACE_OPS, length, [out_block(0)] + [anywhere] * (len(given) - 1),
            out_block(at), jax.ShapeDtypeStruct((1, length, width), bf16), [], {1: 0} if len(given) > 1 else {},
        )(*given)
    return handed


def solution(mesh):
    in_specs = (
        P("pipe", None, "seq", None),
        P("pipe", None, None, None),
        P("pipe", None, None),
        P("pipe", None, None),
        P("pipe", None),
    )
    out_specs = P("pipe", "seq", None)
    return jax.shard_map(shards, mesh=mesh, in_specs=in_specs, out_specs=out_specs, check_vma=False)
```

time: 288 us -> 79 us (0.27); the launches traced: 282 us -> 78.4 us
  matrix products: 92.6 us -> 0 us
  blocking collectives: 54.5 us -> 0 us
  local copies, waits for them, and re-layouts: 40.2 us -> 1.06 us
  waiting for transfers between devices: 53 us -> 25.7 us
  Pallas kernels: 0 us -> 26.5 us
  other arithmetic: 21.6 us -> 0.17 us
  starting transfers between devices: 16.9 us -> 24.9 us
  loops' own time: 2.92 us -> 0 us
    dot_general x24 -> x0, matrix products: 92.6 us -> none  [the longest x2 37.8 us: one_block(): jnp.einsum('qr,krc->kqc', inner_sin, turned_real, precision=highest)]
    all_to_all x1 -> x0, blocking collectives: 54.5 us -> none  [spectral_mix(): lax.all_to_all(mixed.reshape(total, share), 'seq', split_axis=0, concat_a...]
    pallas_call x0 -> x9, Pallas kernels: none -> 26.5 us  [the longest x2 11.9 us: local_mix(): call(functools.partial(mix_kernel, order, length, length, total), 'local_...]
    all_to_all x1 -> x2, waiting for transfers between devices: 25.9 us -> 5.39 us  [shards(): to_all = lambda x: lax.all_to_all(x, 'seq', 0, 0, tiled=True)]
    add x3 -> x0, other arithmetic: 11.3 us -> none  [the longest x1 9.39 us: shards(): featured + short_filter[:, :, offset, None, :] * extended[:, :, TAPS - 1...]
    sub x4 -> x0, local copies, waits for them, and re-layouts: 10.8 us -> none  [the longest x2 6.14 us: one_block(): reverted_real = back_real * twist_cos - back_imag * twist_sin]
    convert_element_type x5 -> x0, other arithmetic: 8.09 us -> none  [the longest x1 4.08 us: shards(): extended = jnp.concatenate([before, projected], axis=2).astype(jnp.float32)]
    add x4 -> x0, local copies, waits for them, and re-layouts: 7.87 us -> none  [the longest x2 4.05 us: one_block(): reverted_imag = back_imag * twist_cos + back_real * twist_sin]
  transfers between devices with their start and end apart: 3 -> 5, of which waited for: 2 -> 4; matrix products, arithmetic and copies ran while one was open for 2% -> 0% of each run, Pallas kernels for 0% -> 27%
where the time goes in v3:
time: 79 us; the launch traced here: 78.4 us
  Pallas kernels  26.5 us (34%)
  waiting for transfers between devices  25.7 us (33%)
  starting transfers between devices  24.9 us (32%)
  local copies, waits for them, and re-layouts  1.06 us (1%)
    ppermute x2, waiting for transfers between devices, shards(): came = lax.ppermute(output, 'pipe', onward)  20.3 us
    all_to_all x2, starting transfers between devices, shards(): to_all = lambda x: lax.all_to_all(x, 'seq', 0, 0, tiled=True)  16.4 us
    pallas_call x2, Pallas kernels, local_mix(): call(functools.partial(mix_kernel, order, length, length, total), 'local_...  11.9 us
    ppermute x2, starting transfers between devices, shards(): came = lax.ppermute(output, 'pipe', onward)  6.8 us
    pallas_call x2, Pallas kernels, shards(): call(functools.partial(finish_kernel, order, length, total), 'finished',...  6.3 us
    all_to_all x2, waiting for transfers between devices, shards(): to_all = lambda x: lax.all_to_all(x, 'seq', 0, 0, tiled=True)  5.39 us
    pallas_call x1, Pallas kernels, shards(): pl.pallas_call(functools.partial(state_kernel, order, length, pitch, tota...  5.06 us
    ppermute x1, starting transfers between devices, shards(): lax.ppermute(projected[:, :, length - (TAPS - 1):, :], 'seq', [(i, i + 1)...  1.74 us
  transfers between devices with their start and end apart: 5, of which 4 were waited for; matrix products, arithmetic and copies ran while one was open for 0% of the time, Pallas kernels for 27%

profile of v3, /device:TPU:32, one launch (start us, length us, event | category | flops | bytes accessed | tf_op | source)
XLA Modules:
  0.0 78.4 jit_solution(13428019019633535165)
XLA Ops:
  0.0 0.0 copy-start
  0.0 0.0 copy-start.2
  0.0 0.0 copy-start.3
  0.0 1.0 %slice.3 = bf16[1,3,2,4096]{3,2,1,0:T(2,128)(2,1)S(1)} slice(bf16[1,3,128,4096]{3,2,1,0:T(8,128)(2,1)} %inputs.5), slice={[0:1], [0:3], [126:128], [0:4096]} | slice | bytes 98304 | tf_op jit(solution)/shard_map/slice | solution.py:226
  1.1 1.7 %collective-permute-start = (bf16[1,3,2,4096]{3,2,1,0:T(2,128)(2,1)S(1)}, bf16[1,3,2,4096]{3,2,1,0:T(2,128)(2,1)S(1)}, u32[]{:S(2)}, u32[]{:S(2)}) collective-permute-start(bf16[1,3,2,4096]{3,2,1,0:T(2,128)(2,1)S(1)} %slice.3), channel_id=1, source_target_pairs={{0,32},{32,64},{64,96},{96,128},{128,160},{160,192},{192,224},{224... | collective-permute-start | bytes 147464 | tf_op jit(solution)/shard_map/ppermute | solution.py:226
  2.8 5.1 %local_states.1 = (f32[16,32,128]{2,1,0:T(8,128)S(1)}, f32[16,32,128]{2,1,0:T(8,128)S(1)}, f32[4,32,128]{2,1,0:T(8,128)S(1)}, bf16[4,64,16,128]{3,2,1,0:T(8,128)(2,1)S(1)}) custom-call(bf16[1,3,128,4096]{3,2,1,0:T(8,128)(2,1)} %inputs.5, f32[9,32,128]{2,1,0:T(8,128)} %bitcast.4, f32[1,16,4096]{2,1,0:T(8,128)} %rates.7), custom_call_target="tpu_custom_call" | custom-call | flops 28835840 | bytes 4194304 | tf_op jit(solution)/shard_map/local_states/pallas_call | solution.py:237
  7.9 0.0 collective-permute-done.rim
  7.9 0.0 copy-done.2
  7.9 0.8 %first_tokens.1 = (bf16[16,32,128]{2,1,0:T(8,128)(2,1)}, f32[4,32,128]{2,1,0:T(8,128)S(1)}) custom-call(bf16[1,3,2,4096]{3,2,1,0:T(2,128)(2,1)S(1)} %collective-permute-done.rim, f32[4,32,128]{2,1,0:T(8,128)S(1)} %get-tuple-element.27.head, f32[9,32,128]{2,1,0:T(8,128)S(1)} %bitcast.7, f32[16,32,128]{2,1,0:T(8,128)S(1)} %get-tuple-element.28.ends, ...), custom_call_target="tpu_custom_call" | custom-call | tf_op jit(solution)/shard_map/first_tokens/pallas_call | solution.py:256
  8.7 11.8 %all-to-all-start = ((bf16[16,32,128]{2,1,0:T(8,128)(2,1)}), bf16[16,32,128]{2,1,0:T(8,128)(2,1)S(1)}, u32[]{:S(2)}, u32[]{:S(2)}) async-start(bf16[16,32,128]{2,1,0:T(8,128)(2,1)} %get-tuple-element.32), calls=%async_computation | async-start | bytes 262144 | tf_op jit(solution)/shard_map/all_to_all | solution.py:223
  20.5 0.0 copy-done
  20.5 0.0 copy-done.3
  20.5 0.2 multiply_bitcast_fusion.scaled
  20.7 5.9 %local_mix.2 = (f32[2,128,8,128]{3,2,1,0:T(8,128)}, f32[2,128,8,128]{3,2,1,0:T(8,128)}) custom-call(bf16[1,3,128,4096]{3,2,1,0:T(8,128)(2,1)} %inputs.5, f32[9,32,128]{2,1,0:T(8,128)} %bitcast.5, bf16[4,64,16,128]{3,2,1,0:T(8,128)(2,1)S(1)} %get-tuple-element.41.gate, f32[4,32,128]{2,1,0:T(8,128)S(1)} %get-tuple-element.34.edge, f32[1,16,4096]{2,1,0:T(8,128)} %rates.7, ...), custom_call_target="tpu_custom_call" | custom-call | flops 20971520 | bytes 2097152 | tf_op jit(solution)/shard_map/local_mix/pallas_call | solution.py:268
  26.6 0.0 copy-start.1
  26.6 2.6 %all-to-all-done.came = bf16[16,32,128]{2,1,0:T(8,128)(2,1)S(1)} async-done(((bf16[16,32,128]{2,1,0:T(8,128)(2,1)}), bf16[16,32,128]{2,1,0:T(8,128)(2,1)S(1)}, u32[]{:S(2)}, u32[]{:S(2)}) %all-to-all-start) | async-done | bytes 131104 | tf_op jit(solution)/shard_map/all_to_all | solution.py:223
  29.3 0.7 scan_chunks.1
  30.0 4.6 %all-to-all-start.1 = ((bf16[16,32,128]{2,1,0:T(8,128)(2,1)}), bf16[16,32,128]{2,1,0:T(8,128)(2,1)S(1)}, u32[]{:S(2)}, u32[]{:S(2)}) async-start(bf16[16,32,128]{2,1,0:T(8,128)(2,1)} %scan_chunks.1), calls=%async_computation.1 | async-start | bytes 262144 | tf_op jit(solution)/shard_map/all_to_all | solution.py:223
  34.6 6.0 %local_mix.3 = (f32[2,128,8,128]{3,2,1,0:T(8,128)}, f32[2,128,8,128]{3,2,1,0:T(8,128)}) custom-call(bf16[1,3,128,4096]{3,2,1,0:T(8,128)(2,1)} %inputs.5, f32[9,32,128]{2,1,0:T(8,128)} %bitcast.6, bf16[4,64,16,128]{3,2,1,0:T(8,128)(2,1)S(1)} %get-tuple-element.41.gate, f32[4,32,128]{2,1,0:T(8,128)S(1)} %get-tuple-element.34.edge, f32[1,16,4096]{2,1,0:T(8,128)} %rates.7, ...), custom_call_target="tpu_custom_call" | custom-call | flops 20971520 | bytes 2097152 | tf_op jit(solution)/shard_map/local_mix/pallas_call | solution.py:268
  40.5 2.8 %all-to-all-done.1.start = bf16[16,32,128]{2,1,0:T(8,128)(2,1)S(1)} async-done(((bf16[16,32,128]{2,1,0:T(8,128)(2,1)}), bf16[16,32,128]{2,1,0:T(8,128)(2,1)S(1)}, u32[]{:S(2)}, u32[]{:S(2)}) %all-to-all-start.1) | async-done | bytes 131104 | tf_op jit(solution)/shard_map/all_to_all | solution.py:223
  43.3 0.0 copy-done.1
  43.3 3.1 %finished.3 = bf16[1,128,2048]{2,1,0:T(8,128)(2,1)S(1)} custom-call(f32[2,128,8,128]{3,2,1,0:T(8,128)} %get-tuple-element.47.lead, f32[2,128,8,128]{3,2,1,0:T(8,128)} %get-tuple-element.48.mix, f32[1,16,4096]{2,1,0:T(8,128)S(1)} %copy-done.1, f32[16,4096]{1,0:T(8,128)S(1)} %multiply_bitcast_fusion.scaled, bf16[16,32,128]{2,1,0:T(8,128)(2,1)S(1)} %all-to-all-done.1.start), custom_call_target="tpu_custom_call" | custom-call | flops 10485760 | bytes 2097152 | tf_op jit(solution)/shard_map/finished/pallas_call | solution.py:296
  46.5 3.4 %collective-permute-start.2 = (bf16[1,128,2048]{2,1,0:T(8,128)(2,1)S(1)}, bf16[1,128,2048]{2,1,0:T(8,128)(2,1)S(1)}, u32[]{:S(2)}, u32[]{:S(2)}) collective-permute-start(bf16[1,128,2048]{2,1,0:T(8,128)(2,1)S(1)} %finished.3), channel_id=1, source_target_pairs={{0,1},{1,2},{2,3},{3,4},{4,5},{5,6},{6,7},{7,8},{8,9},{9,10},{10,1... | collective-permute-start | bytes 1572872 | tf_op jit(solution)/shard_map/ppermute | solution.py:303
  49.9 3.2 %finished.2 = bf16[1,128,2048]{2,1,0:T(8,128)(2,1)S(1)} custom-call(f32[2,128,8,128]{3,2,1,0:T(8,128)} %get-tuple-element.44.lead, f32[2,128,8,128]{3,2,1,0:T(8,128)} %get-tuple-element.45.mix, f32[1,16,4096]{2,1,0:T(8,128)S(1)} %copy-done.1, f32[16,4096]{1,0:T(8,128)S(1)} %multiply_bitcast_fusion.scaled, bf16[16,32,128]{2,1,0:T(8,128)(2,1)S(1)} %all-to-all-done.1.start), custom_call_target="tpu_custom_call" | custom-call | flops 10485760 | bytes 2097152 | tf_op jit(solution)/shard_map/finished/pallas_call | solution.py:296
  53.0 3.4 %collective-permute-start.1 = (bf16[1,128,2048]{2,1,0:T(8,128)(2,1)S(1)}, bf16[1,128,2048]{2,1,0:T(8,128)(2,1)S(1)}, u32[]{:S(2)}, u32[]{:S(2)}) collective-permute-start(bf16[1,128,2048]{2,1,0:T(8,128)(2,1)S(1)} %finished.2), channel_id=1, source_target_pairs={{0,1},{1,2},{2,3},{3,4},{4,5},{5,6},{6,7},{7,8},{8,9},{9,10},{10,1... | collective-permute-start | bytes 1572872 | tf_op jit(solution)/shard_map/ppermute | solution.py:303
  56.5 10.0 %collective-permute-done.2.part = bf16[1,128,2048]{2,1,0:T(8,128)(2,1)S(1)} collective-permute-done((bf16[1,128,2048]{2,1,0:T(8,128)(2,1)S(1)}, bf16[1,128,2048]{2,1,0:T(8,128)(2,1)S(1)}, u32[]{:S(2)}, u32[]{:S(2)}) %collective-permute-start.2) | collective-permute-done | bytes 524320 | tf_op jit(solution)/shard_map/ppermute | solution.py:303
  66.5 0.9 %placed.2.rest_0_ = bf16[1,128,4096]{2,1,0:T(8,128)(2,1)} custom-call(bf16[1,128,2048]{2,1,0:T(8,128)(2,1)S(1)} %collective-permute-done.2.part), custom_call_target="tpu_custom_call" | custom-call | flops 2621440000 | bytes 2097152 | tf_op jit(solution)/shard_map/placed/pallas_call | solution.py:305
  67.3 10.2 %collective-permute-done.1.part = bf16[1,128,2048]{2,1,0:T(8,128)(2,1)S(1)} collective-permute-done((bf16[1,128,2048]{2,1,0:T(8,128)(2,1)S(1)}, bf16[1,128,2048]{2,1,0:T(8,128)(2,1)S(1)}, u32[]{:S(2)}, u32[]{:S(2)}) %collective-permute-start.1) | collective-permute-done | bytes 524320 | tf_op jit(solution)/shard_map/ppermute | solution.py:303
  77.6 0.9 %placed.3 = bf16[1,128,4096]{2,1,0:T(8,128)(2,1)} custom-call(bf16[1,128,2048]{2,1,0:T(8,128)(2,1)S(1)} %collective-permute-done.1.part, bf16[1,128,4096]{2,1,0:T(8,128)(2,1)} %placed.2.rest_0_), custom_call_target="tpu_custom_call", output_to_operand_aliasing={{}: (1, {})} | custom-call | flops 2621440000 | bytes 2097152 | tf_op jit(solution)/shard_map/placed/pallas_call | solution.py:305
Async XLA Ops:
  0.0 20.5 %copy-start = (f32[1,16,4096]{2,1,0:T(8,128)S(1)}, f32[1,16,4096]{2,1,0:T(8,128)}, u32[]{:S(2)}) copy-start(f32[1,16,4096]{2,1,0:T(8,128)} %rates.7) | copy-start | bytes 786436
  0.0 7.9 %copy-start.2 = (f32[1,3,3,4096]{3,0,2,1:T(1,128)S(1)}, f32[1,3,3,4096]{3,0,2,1:T(1,128)}, u32[]{:S(2)}) copy-start(f32[1,3,3,4096]{3,0,2,1:T(1,128)} %param.6) | copy-start | bytes 442372
  0.0 20.5 %copy-start.3 = (f32[1,16,4096]{2,1,0:T(8,128)S(1)}, f32[1,16,4096]{2,1,0:T(8,128)}, u32[]{:S(2)}) copy-start(f32[1,16,4096]{2,1,0:T(8,128)} %param.8) | copy-start | bytes 786436
  1.1 6.8 %collective-permute-start = (bf16[1,3,2,4096]{3,2,1,0:T(2,128)(2,1)S(1)}, bf16[1,3,2,4096]{3,2,1,0:T(2,128)(2,1)S(1)}, u32[]{:S(2)}, u32[]{:S(2)}) collective-permute-start(bf16[1,3,2,4096]{3,2,1,0:T(2,128)(2,1)S(1)} %slice.3), channel_id=1, source_target_pairs={{0,32},{32,64},{64,96},{96,128},{128,160},{160,192},{192,224},{224... | collective-permute-start | bytes 147464 | tf_op jit(solution)/shard_map/ppermute | solution.py:226
  8.7 20.5 %all-to-all-start = ((bf16[16,32,128]{2,1,0:T(8,128)(2,1)}), bf16[16,32,128]{2,1,0:T(8,128)(2,1)S(1)}, u32[]{:S(2)}, u32[]{:S(2)}) async-start(bf16[16,32,128]{2,1,0:T(8,128)(2,1)} %get-tuple-element.32), calls=%async_computation | async-start | bytes 262144 | tf_op jit(solution)/shard_map/all_to_all | solution.py:223
  26.6 16.7 %copy-start.1 = (f32[1,16,4096]{2,1,0:T(8,128)S(1)}, f32[1,16,4096]{2,1,0:T(8,128)}, u32[]{:S(2)}) copy-start(f32[1,16,4096]{2,1,0:T(8,128)} %rates.7) | copy-start | bytes 786436
  30.0 13.4 %all-to-all-start.1 = ((bf16[16,32,128]{2,1,0:T(8,128)(2,1)}), bf16[16,32,128]{2,1,0:T(8,128)(2,1)S(1)}, u32[]{:S(2)}, u32[]{:S(2)}) async-start(bf16[16,32,128]{2,1,0:T(8,128)(2,1)} %scan_chunks.1), calls=%async_computation.1 | async-start | bytes 262144 | tf_op jit(solution)/shard_map/all_to_all | solution.py:223
  46.5 20.0 %collective-permute-start.2 = (bf16[1,128,2048]{2,1,0:T(8,128)(2,1)S(1)}, bf16[1,128,2048]{2,1,0:T(8,128)(2,1)S(1)}, u32[]{:S(2)}, u32[]{:S(2)}) collective-permute-start(bf16[1,128,2048]{2,1,0:T(8,128)(2,1)S(1)} %finished.3), channel_id=1, source_target_pairs={{0,1},{1,2},{2,3},{3,4},{4,5},{5,6},{6,7},{7,8},{8,9},{9,10},{10,1... | collective-permute-start | bytes 1572872 | tf_op jit(solution)/shard_map/ppermute | solution.py:303
  53.0 24.5 %collective-permute-start.1 = (bf16[1,128,2048]{2,1,0:T(8,128)(2,1)S(1)}, bf16[1,128,2048]{2,1,0:T(8,128)(2,1)S(1)}, u32[]{:S(2)}, u32[]{:S(2)}) collective-permute-start(bf16[1,128,2048]{2,1,0:T(8,128)(2,1)S(1)} %finished.2), channel_id=1, source_target_pairs={{0,1},{1,2},{2,3},{3,4},{4,5},{5,6},{6,7},{7,8},{8,9},{9,10},{10,1... | collective-permute-start | bytes 1572872 | tf_op jit(solution)/shard_map/ppermute | solution.py:303

commit v4 on v3

--- a/solution.py
+++ b/solution.py
@@ -11,8 +11,9 @@
 LANES = 128
 ROWS = 8
 GROUP = ROWS * LANES
-PARTS = 2
+EARLY = 2
 PLACE_OPS = 10000
+PIECES = 4
 f32 = jnp.float32
 bf16 = jnp.bfloat16
 
@@ -99,7 +100,7 @@
                 states = tuple(s * x + gated for s, x in zip(steps, states))
             return states
 
-        states = lax.fori_loop(1, length // 2, state_step, (zero,) * order, unroll=3)
+        states = lax.fori_loop(1, length // 2, state_step, (zero,) * order, unroll=9)
         for n in range(order):
             end_ref[n, at, :] = states[n]
 
@@ -157,23 +158,81 @@
         return tokens(pair, states, (both[:ROWS], both[ROWS:]))
 
     states = tokens(0, (jnp.zeros((ROWS, LANES), f32),) * order, (edge[2], edge[3]))
-    lax.fori_loop(1, length // 2, step, states)
-
-
-def finish_kernel(order, length, total, lead, mix, rates, scaled, start, out_ref, rows, mode_rows, start_rows):
+    lax.fori_loop(1, length // 2, step, states, unroll=3)
+
+
+def finish_kernel(order, length, pitch, total, first, count, *refs):
+    sources, (rates, scaled, start, out_ref, parts, rows, mode_rows, sems) = refs[: 2 * count], refs[2 * count :]
+    piece = length // PIECES
+
+    def fetch(g, i, c):
+        which, at = 2 * g + i, pl.ds(c * piece, piece)
+        return pltpu.make_async_copy(sources[which].at[0, at], parts.at[which, at], sems.at[which, c])
+
+    for g in range(count):
+        for c in range(PIECES):
+            for i in range(2):
+                fetch(g, i, c).start()
+    for g in range(count):
+        lanes = slice((first + g) * GROUP, (first + g + 1) * GROUP)
+        steps = [jnp.exp(-(rate / total)) for rate in by_mode(mode_rows, rates[0, :, lanes], order)]
+        scales = by_mode(mode_rows, scaled[:, lanes], order)
+        pair = (first + g) // 2 * 2 * ROWS
+        states = start[:, pair : pair + 2 * ROWS, :].astype(f32)
+        states = states[:, (first + g) % 2 * ROWS : ((first + g) % 2 + 1) * ROWS]
+
+        def step(t, terms):
+            terms = tuple(s * x for s, x in zip(steps, terms))
+            rows[pl.ds(t, ROWS, stride=pitch), :] = parts[2 * g, t] * (parts[2 * g + 1, t] + tree_sum(list(terms)))
+            return terms
+
+        terms = tuple(scales[n] * states[n] for n in range(order))
+        for c in range(PIECES):
+            for i in range(2):
+                fetch(g, i, c).wait()
+            terms = lax.fori_loop(c * piece, (c + 1) * piece, step, terms, unroll=8)
+        for k in range(ROWS):
+            lanes = slice(g * GROUP + k * LANES, g * GROUP + (k + 1) * LANES)
+            out_ref[0, :, lanes] = rows[pl.ds(k * pitch, length), :].astype(bf16)
+
+
+def whole_kernel(order, length, pitch, total, odd, inputs, taps, gate, edge, rates, scaled, skip, start, out_ref,
+                 raw, rows, mode_rows, start_rows):
     steps = [jnp.exp(-(rate / total)) for rate in by_mode(mode_rows, rates[0], order)]
     scales = by_mode(mode_rows, scaled[...], order)
     start_rows[...] = start[...].astype(f32)
-    at = pl.ds(pl.multiple_of(pl.program_id(0) * ROWS, ROWS), ROWS)
-
-    def step(t, terms):
-        terms = tuple(s * x for s, x in zip(steps, terms))
-        rows[pl.ds(t, ROWS, stride=length), :] = lead[0, t] * (mix[0, t] + tree_sum(list(terms)))
-        return terms
-
-    lax.fori_loop(0, length, step, tuple(scales[n] * start_rows[n, at, :] for n in range(order)), unroll=4)
+    at = pl.ds(odd * ROWS, ROWS)
+    weights = [taps[a] for a in range(TAPS)]
     for k in range(ROWS):
-        out_ref[0, :, pl.ds(k * LANES, LANES)] = rows[pl.ds(k * length, length), :].astype(bf16)
+        raw[pl.ds(k * pitch, length), :] = inputs[0, 0, :, k * LANES : (k + 1) * LANES].astype(f32)
+
+    def lead_step(pair, before):
+        for sub in range(2):
+            t = 2 * pair + sub
+            one, two = before
+            now = raw[pl.ds(t, ROWS, stride=pitch), :]
+            rows[pl.ds(t, ROWS, stride=pitch), :] = weights[0] * now + weights[1] * one + weights[2] * two
+            before = (now, one)
+        return before
+
+    lax.fori_loop(0, length // 2, lead_step, (edge[1], edge[0]), unroll=4)
+
+    def tokens(pair, states, both):
+        for sub, gated in enumerate(both):
+            t = 2 * pair + sub
+            states = tuple(s * x + gated for s, x in zip(steps, states))
+            mixed = tree_sum([w * x for w, x in zip(scales, states)]) + skip[...] * gated
+            raw[pl.ds(t, ROWS, stride=pitch), :] = rows[pl.ds(t, ROWS, stride=pitch), :] * mixed
+        return states
+
+    def step(pair, states):
+        both = gate[0, pair].astype(f32)
+        return tokens(pair, states, (both[:ROWS], both[ROWS:]))
+
+    states = tokens(0, tuple(start_rows[n, at, :] for n in range(order)), (edge[2], edge[3]))
+    lax.fori_loop(1, length // 2, step, states, unroll=3)
+    for k in range(ROWS):
+        out_ref[0, :, pl.ds(k * LANES, LANES)] = raw[pl.ds(k * pitch, length), :].astype(bf16)
 
 
 def place_kernel(part, *rest):
@@ -261,25 +320,21 @@
         name="first_tokens",
     )(rim, head, taps, ends, span)
 
-    share = groups // PARTS
-
-    def local_mix(part, gated):
-        at = part * share
+    def local_mix(at, gated):
         return call(
-            functools.partial(mix_kernel, order, length, length, total), "local_mix", share, 80, length,
+            functools.partial(mix_kernel, order, length, pitch, total), "local_mix", 1, 80, length,
             [pl.BlockSpec((1, 1, length, GROUP), lambda g: (0, 0, 0, at + g)), stack(TAPS, at),
              pairs(at), stack(4, at), rate_block(at), scale_block(at),
              pl.BlockSpec((ROWS, LANES), lambda g: (at + g, 0))],
-            [tokens(0), tokens(0)], [pltpu.HBM((share, length, ROWS, LANES), f32)] * 2,
-            [pltpu.VMEM((ROWS * length, LANES), f32), mode_rows],
+            [tokens(0), tokens(0)], [pltpu.HBM((1, length, ROWS, LANES), f32)] * 2,
+            [pltpu.VMEM((ROWS * pitch, LANES), f32), mode_rows],
         )(held(projected), held(taps), gated, edge, held(decay_rate), scaled, held(skip))
 
-    mixes = [None] * PARTS
     wire, gate, residue = after(wire, gate, residue)
     scaled = residue[0] * jnp.sqrt(-jnp.expm1(-2.0 * (decay_rate[0] / total)))
     came = to_all(wire)
-    mixes[0] = local_mix(0, gate)
-    came, mixes[0], gate = after(came, mixes[0], gate)
+    mixes = [local_mix(0, gate)]
+    came, mixes, gate = after(came, mixes, gate)
     enter = pl.pallas_call(
         scan_kernel,
         out_shape=jax.ShapeDtypeStruct(came.shape, bf16),
@@ -288,22 +343,45 @@
     )(came, span)
     enter, gate = after(enter, gate)
     start = to_all(enter)
-    mixes[1] = local_mix(1, gate)
-    start, mixes[1] = after(start, mixes[1])
+    mixes.append(local_mix(1, gate))
+    start, mixes, gate = after(start, mixes, gate)
+    in_vmem = pl.BlockSpec(memory_space=pltpu.VMEM)
+    share = jax.ShapeDtypeStruct((1, length, GROUP), bf16)
     handed = None
-    for part in range(PARTS):
-        at = part * share
-        output = call(
-            functools.partial(finish_kernel, order, length, total), "finished", share, 40, length,
-            [tokens(0), tokens(0), rate_block(at), scale_block(at),
-             pl.BlockSpec((order, share * ROWS, LANES), lambda g, part=part: (0, part, 0))],
-            out_block(0), jax.ShapeDtypeStruct((1, length, share * GROUP), bf16),
-            [pltpu.VMEM((ROWS * length, LANES), f32), mode_rows, pltpu.VMEM((order, share * ROWS, LANES), f32)],
-        )(*map(held, mixes[part]), decay_rate, scaled, start)
+    for at in range(groups):
+        if at < EARLY:
+            output = pl.pallas_call(
+                functools.partial(finish_kernel, order, length, pitch, total, at, 1),
+                in_specs=[anywhere] * 2 + [in_vmem] * 3,
+                out_specs=in_vmem,
+                out_shape=share,
+                scratch_shapes=[
+                    pltpu.VMEM((2, length, ROWS, LANES), f32),
+                    pltpu.VMEM((ROWS * pitch, LANES), f32),
+                    mode_rows,
+                    pltpu.SemaphoreType.DMA((2, PIECES)),
+                ],
+                compiler_params=pltpu.CompilerParams(vmem_limit_bytes=16 << 20),
+                cost_estimate=pl.CostEstimate(
+                    flops=40 * length * GROUP, bytes_accessed=8 * length * GROUP, transcendentals=0
+                ),
+                name="finished",
+            )(*map(held, mixes[at]), decay_rate, scaled, start)
+        else:
+            output = call(
+                functools.partial(whole_kernel, order, length, pitch, total, at % 2), "mixed_output", 1, 90, length,
+                [pl.BlockSpec((1, 1, length, GROUP), lambda g, at=at: (0, 0, 0, at)), stack(TAPS, at),
+                 pairs(at), stack(4, at), rate_block(at), scale_block(at),
+                 pl.BlockSpec((ROWS, LANES), lambda g, at=at: (at, 0)),
+                 pl.BlockSpec((order, 2 * ROWS, LANES), lambda g, at=at: (0, at // 2, 0))],
+                out_block(0), share,
+                [pltpu.VMEM((ROWS * pitch, LANES), f32)] * 2
+                + [mode_rows, pltpu.VMEM((order, 2 * ROWS, LANES), f32)],
+            )(held(projected), held(taps), gate, edge, held(decay_rate), scaled, held(skip), start)
         came = lax.ppermute(output, "pipe", onward)
         given = [came] if handed is None else [came, handed]
         handed = call(
-            place_kernel, "placed", share, PLACE_OPS, length, [out_block(0)] + [anywhere] * (len(given) - 1),
+            place_kernel, "placed", 1, PLACE_OPS, length, [out_block(0)] + [anywhere] * (len(given) - 1),
             out_block(at), jax.ShapeDtypeStruct((1, length, width), bf16), [], {1: 0} if len(given) > 1 else {},
         )(*given)
     return handed

time: 79 us -> 75.9 us (0.961)
  waiting for transfers between devices: 25.7 us -> 19.3 us
  starting transfers between devices: 24.9 us -> 29.4 us
  Pallas kernels: 26.5 us -> 25.3 us
    ppermute x2 -> x4, waiting for transfers between devices: 20.3 us -> 8.9 us  [shards(): came = lax.ppermute(output, 'pipe', onward)]
    ppermute x2 -> x4, starting transfers between devices: 6.8 us -> 12.4 us  [shards(): came = lax.ppermute(output, 'pipe', onward)]
    all_to_all x2, waiting for transfers between devices: 5.39 us -> 10.4 us  [shards(): to_all = lambda x: lax.all_to_all(x, 'seq', 0, 0, tiled=True)]
    pallas_call x6 -> x10, Pallas kernels: 19.9 us -> 18.8 us  [the longest x2 6.86 us: local_mix(): call(functools.partial(mix_kernel, order, length, pitch, total), 'local_m...]
    all_to_all x2, starting transfers between devices: 16.4 us -> 15.3 us  [shards(): to_all = lambda x: lax.all_to_all(x, 'seq', 0, 0, tiled=True)]
  transfers between devices with their start and end apart: 5 -> 7, of which waited for: 4 -> 4; matrix products, arithmetic and copies ran while one was open for 0% -> 0% of each run, Pallas kernels for 27% -> 28%
where the time goes in v4:
time: 75.9 us; the launch traced here: 75.4 us
  starting transfers between devices  29.4 us (39%)
  Pallas kernels  25.3 us (33%)
  waiting for transfers between devices  19.3 us (25%)
  local copies, waits for them, and re-layouts  1.06 us (1%)
    all_to_all x2, starting transfers between devices, shards(): to_all = lambda x: lax.all_to_all(x, 'seq', 0, 0, tiled=True)  15.3 us
    ppermute x4, starting transfers between devices, shards(): came = lax.ppermute(output, 'pipe', onward)  12.4 us
    all_to_all x2, waiting for transfers between devices, shards(): to_all = lambda x: lax.all_to_all(x, 'seq', 0, 0, tiled=True)  10.4 us
    ppermute x4, waiting for transfers between devices, shards(): came = lax.ppermute(output, 'pipe', onward)  8.9 us
    pallas_call x2, Pallas kernels, local_mix(): call(functools.partial(mix_kernel, order, length, pitch, total), 'local_m...  6.86 us
    pallas_call x2, Pallas kernels, shards(): call(functools.partial(whole_kernel, order, length, pitch, total, at % 2)...  5.5 us
    pallas_call x1, Pallas kernels, shards(): pl.pallas_call(functools.partial(state_kernel, order, length, pitch, tota...  4.96 us
    pallas_call x2, Pallas kernels, shards(): pl.pallas_call(functools.partial(finish_kernel, order, length, pitch, tot...  3.54 us
  transfers between devices with their start and end apart: 7, of which 4 were waited for; matrix products, arithmetic and copies ran while one was open for 0% of the time, Pallas kernels for 28%

profile of v4, /device:TPU:32, one launch (start us, length us, event | category | flops | bytes accessed | tf_op | source)
XLA Modules:
  0.0 75.4 jit_solution(5960948699818544917)
XLA Ops:
  0.0 1.0 %slice.3 = bf16[1,3,2,4096]{3,2,1,0:T(2,128)(2,1)S(1)} slice(bf16[1,3,128,4096]{3,2,1,0:T(8,128)(2,1)} %inputs.9), slice={[0:1], [0:3], [126:128], [0:4096]} | slice | bytes 98304 | tf_op jit(solution)/shard_map/slice | solution.py:285
  1.1 1.7 %collective-permute-start = (bf16[1,3,2,4096]{3,2,1,0:T(2,128)(2,1)S(1)}, bf16[1,3,2,4096]{3,2,1,0:T(2,128)(2,1)S(1)}, u32[]{:S(2)}, u32[]{:S(2)}) collective-permute-start(bf16[1,3,2,4096]{3,2,1,0:T(2,128)(2,1)S(1)} %slice.3), channel_id=1, source_target_pairs={{0,32},{32,64},{64,96},{96,128},{128,160},{160,192},{192,224},{224... | collective-permute-start | bytes 147464 | tf_op jit(solution)/shard_map/ppermute | solution.py:285
  2.8 5.0 %local_states.1 = (f32[16,32,128]{2,1,0:T(8,128)S(1)}, f32[16,32,128]{2,1,0:T(8,128)S(1)}, f32[4,32,128]{2,1,0:T(8,128)S(1)}, bf16[4,64,16,128]{3,2,1,0:T(8,128)(2,1)S(1)}) custom-call(bf16[1,3,128,4096]{3,2,1,0:T(8,128)(2,1)} %inputs.9, f32[9,32,128]{2,1,0:T(8,128)} %bitcast.4, f32[1,16,4096]{2,1,0:T(8,128)} %refs_2_.3), custom_call_target="tpu_custom_call" | custom-call | flops 28835840 | bytes 4194304 | tf_op jit(solution)/shard_map/local_states/pallas_call | solution.py:296
  7.8 0.0 collective-permute-done.rim
  7.8 0.0 copy-done.2
  7.8 0.8 %first_tokens.1 = (bf16[16,32,128]{2,1,0:T(8,128)(2,1)}, f32[4,32,128]{2,1,0:T(8,128)S(1)}) custom-call(bf16[1,3,2,4096]{3,2,1,0:T(2,128)(2,1)S(1)} %collective-permute-done.rim, f32[4,32,128]{2,1,0:T(8,128)S(1)} %get-tuple-element.30.head, f32[9,32,128]{2,1,0:T(8,128)S(1)} %bitcast.9, f32[16,32,128]{2,1,0:T(8,128)S(1)} %get-tuple-element.31.ends, ...), custom_call_target="tpu_custom_call" | custom-call | tf_op jit(solution)/shard_map/first_tokens/pallas_call | solution.py:315
  8.6 11.8 %all-to-all-start = ((bf16[16,32,128]{2,1,0:T(8,128)(2,1)}), bf16[16,32,128]{2,1,0:T(8,128)(2,1)S(1)}, u32[]{:S(2)}, u32[]{:S(2)}) async-start(bf16[16,32,128]{2,1,0:T(8,128)(2,1)} %get-tuple-element.35), calls=%async_computation | async-start | bytes 262144 | tf_op jit(solution)/shard_map/all_to_all | solution.py:282
  20.4 0.0 copy-done
  20.4 0.0 copy-done.3
  20.4 0.2 multiply_bitcast_fusion.scaled.refs_3_
  20.6 3.4 %local_mix.2 = (f32[1,128,8,128]{3,2,1,0:T(8,128)}, f32[1,128,8,128]{3,2,1,0:T(8,128)}) custom-call(bf16[1,3,128,4096]{3,2,1,0:T(8,128)(2,1)} %inputs.9, f32[9,32,128]{2,1,0:T(8,128)} %bitcast.5, bf16[4,64,16,128]{3,2,1,0:T(8,128)(2,1)S(1)} %get-tuple-element.49.gate, f32[4,32,128]{2,1,0:T(8,128)S(1)} %get-tuple-element.37.edge, f32[1,16,4096]{2,1,0:T(8,128)} %refs_2_.3, ...), custom_call_target="tpu_custom_call" | custom-call | flops 10485760 | bytes 1048576 | tf_op jit(solution)/shard_map/local_mix/pallas_call | solution.py:324
  24.0 5.1 %all-to-all-done.came = bf16[16,32,128]{2,1,0:T(8,128)(2,1)S(1)} async-done(((bf16[16,32,128]{2,1,0:T(8,128)(2,1)}), bf16[16,32,128]{2,1,0:T(8,128)(2,1)S(1)}, u32[]{:S(2)}, u32[]{:S(2)}) %all-to-all-start) | async-done | bytes 131104 | tf_op jit(solution)/shard_map/all_to_all | solution.py:282
  29.2 0.7 scan_chunks.1
  29.9 3.5 %all-to-all-start.1 = ((bf16[16,32,128]{2,1,0:T(8,128)(2,1)}), bf16[16,32,128]{2,1,0:T(8,128)(2,1)S(1)}, u32[]{:S(2)}, u32[]{:S(2)}) async-start(bf16[16,32,128]{2,1,0:T(8,128)(2,1)} %scan_chunks.1), calls=%async_computation.1 | async-start | bytes 262144 | tf_op jit(solution)/shard_map/all_to_all | solution.py:282
  33.4 3.4 %local_mix.3 = (f32[1,128,8,128]{3,2,1,0:T(8,128)}, f32[1,128,8,128]{3,2,1,0:T(8,128)}) custom-call(bf16[1,3,128,4096]{3,2,1,0:T(8,128)(2,1)} %inputs.9, f32[9,32,128]{2,1,0:T(8,128)} %bitcast.6, bf16[4,64,16,128]{3,2,1,0:T(8,128)(2,1)S(1)} %get-tuple-element.49.gate, f32[4,32,128]{2,1,0:T(8,128)S(1)} %get-tuple-element.37.edge, f32[1,16,4096]{2,1,0:T(8,128)} %refs_2_.3, ...), custom_call_target="tpu_custom_call" | custom-call | flops 10485760 | bytes 1048576 | tf_op jit(solution)/shard_map/local_mix/pallas_call | solution.py:324
  36.8 5.2 %all-to-all-done.1.start.refs_4_ = bf16[16,32,128]{2,1,0:T(8,128)(2,1)S(1)} async-done(((bf16[16,32,128]{2,1,0:T(8,128)(2,1)}), bf16[16,32,128]{2,1,0:T(8,128)(2,1)S(1)}, u32[]{:S(2)}, u32[]{:S(2)}) %all-to-all-start.1) | async-done | bytes 131104 | tf_op jit(solution)/shard_map/all_to_all | solution.py:282
  42.0 1.8 %finished.3 = bf16[1,128,1024]{2,1,0:T(8,128)(2,1)S(1)} custom-call(f32[1,128,8,128]{3,2,1,0:T(8,128)} %get-tuple-element.53.refs_0_, f32[1,128,8,128]{3,2,1,0:T(8,128)} %get-tuple-element.54.refs_1_, f32[1,16,4096]{2,1,0:T(8,128)S(1)} %copy-done.1, f32[16,4096]{1,0:T(8,128)S(1)} %multiply_bitcast_fusion.scaled.refs_3_, ...), custom_call_target="tpu_custom_call" | custom-call | flops 5242880 | bytes 1048576 | tf_op jit(solution)/shard_map/finished/pallas_call | solution.py:353
  43.8 3.4 %collective-permute-start.4 = (bf16[1,128,1024]{2,1,0:T(8,128)(2,1)S(1)}, bf16[1,128,1024]{2,1,0:T(8,128)(2,1)S(1)}, u32[]{:S(2)}, u32[]{:S(2)}) collective-permute-start(bf16[1,128,1024]{2,1,0:T(8,128)(2,1)S(1)} %finished.3), channel_id=1, source_target_pairs={{0,1},{1,2},{2,3},{3,4},{4,5},{5,6},{6,7},{7,8},{8,9},{9,10},{10,1... | collective-permute-start | bytes 786440 | tf_op jit(solution)/shard_map/ppermute | solution.py:381
  47.2 1.8 %finished.2 = bf16[1,128,1024]{2,1,0:T(8,128)(2,1)S(1)} custom-call(f32[1,128,8,128]{3,2,1,0:T(8,128)} %get-tuple-element.51.refs_0_, f32[1,128,8,128]{3,2,1,0:T(8,128)} %get-tuple-element.52.refs_1_, f32[1,16,4096]{2,1,0:T(8,128)S(1)} %copy-done.1, f32[16,4096]{1,0:T(8,128)S(1)} %multiply_bitcast_fusion.scaled.refs_3_, ...), custom_call_target="tpu_custom_call" | custom-call | flops 5242880 | bytes 1048576 | tf_op jit(solution)/shard_map/finished/pallas_call | solution.py:353
  49.0 3.4 %collective-permute-start.3 = (bf16[1,128,1024]{2,1,0:T(8,128)(2,1)S(1)}, bf16[1,128,1024]{2,1,0:T(8,128)(2,1)S(1)}, u32[]{:S(2)}, u32[]{:S(2)}) collective-permute-start(bf16[1,128,1024]{2,1,0:T(8,128)(2,1)S(1)} %finished.2), channel_id=1, source_target_pairs={{0,1},{1,2},{2,3},{3,4},{4,5},{5,6},{6,7},{7,8},{8,9},{9,10},{10,1... | collective-permute-start | bytes 786440 | tf_op jit(solution)/shard_map/ppermute | solution.py:381
  52.4 2.8 %mixed_output.3 = bf16[1,128,1024]{2,1,0:T(8,128)(2,1)S(1)} custom-call(bf16[1,3,128,4096]{3,2,1,0:T(8,128)(2,1)} %inputs.9, f32[9,32,128]{2,1,0:T(8,128)} %bitcast.7, bf16[4,64,16,128]{3,2,1,0:T(8,128)(2,1)S(1)} %get-tuple-element.49.gate, f32[4,32,128]{2,1,0:T(8,128)S(1)} %get-tuple-element.37.edge, f32[1,16,4096]{2,1,0:T(8,128)} %refs_2_.3, ...), custom_call_target="tpu_custom_call" | custom-call | flops 11796480 | bytes 1048576 | tf_op jit(solution)/shard_map/mixed_output/pallas_call | solution.py:371
  55.2 3.1 %collective-permute-start.2 = (bf16[1,128,1024]{2,1,0:T(8,128)(2,1)S(1)}, bf16[1,128,1024]{2,1,0:T(8,128)(2,1)S(1)}, u32[]{:S(2)}, u32[]{:S(2)}) collective-permute-start(bf16[1,128,1024]{2,1,0:T(8,128)(2,1)S(1)} %mixed_output.3), channel_id=1, source_target_pairs={{0,1},{1,2},{2,3},{3,4},{4,5},{5,6},{6,7},{7,8},{8,9},{9,10},{10,1... | collective-permute-start | bytes 786440 | tf_op jit(solution)/shard_map/ppermute | solution.py:381
  58.3 2.8 %mixed_output.2 = bf16[1,128,1024]{2,1,0:T(8,128)(2,1)S(1)} custom-call(bf16[1,3,128,4096]{3,2,1,0:T(8,128)(2,1)} %inputs.9, f32[9,32,128]{2,1,0:T(8,128)} %bitcast.8, bf16[4,64,16,128]{3,2,1,0:T(8,128)(2,1)S(1)} %get-tuple-element.49.gate, f32[4,32,128]{2,1,0:T(8,128)S(1)} %get-tuple-element.37.edge, f32[1,16,4096]{2,1,0:T(8,128)} %refs_2_.3, ...), custom_call_target="tpu_custom_call" | custom-call | flops 11796480 | bytes 1048576 | tf_op jit(solution)/shard_map/mixed_output/pallas_call | solution.py:371
  61.0 2.5 %collective-permute-start.1 = (bf16[1,128,1024]{2,1,0:T(8,128)(2,1)S(1)}, bf16[1,128,1024]{2,1,0:T(8,128)(2,1)S(1)}, u32[]{:S(2)}, u32[]{:S(2)}) collective-permute-start(bf16[1,128,1024]{2,1,0:T(8,128)(2,1)S(1)} %mixed_output.2), channel_id=1, source_target_pairs={{0,1},{1,2},{2,3},{3,4},{4,5},{5,6},{6,7},{7,8},{8,9},{9,10},{10,1... | collective-permute-start | bytes 786440 | tf_op jit(solution)/shard_map/ppermute | solution.py:381
  63.6 0.0 collective-permute-done.4.part
  63.6 0.7 placed.4.rest_0_
  64.3 0.0 collective-permute-done.3.part
  64.3 0.7 placed.5.rest_0_
  65.0 4.4 %collective-permute-done.2.part = bf16[1,128,1024]{2,1,0:T(8,128)(2,1)S(1)} collective-permute-done((bf16[1,128,1024]{2,1,0:T(8,128)(2,1)S(1)}, bf16[1,128,1024]{2,1,0:T(8,128)(2,1)S(1)}, u32[]{:S(2)}, u32[]{:S(2)}) %collective-permute-start.2) | collective-permute-done | bytes 262176 | tf_op jit(solution)/shard_map/ppermute | solution.py:381
  69.4 0.7 placed.6.rest_0_
  70.1 4.5 %collective-permute-done.1.part = bf16[1,128,1024]{2,1,0:T(8,128)(2,1)S(1)} collective-permute-done((bf16[1,128,1024]{2,1,0:T(8,128)(2,1)S(1)}, bf16[1,128,1024]{2,1,0:T(8,128)(2,1)S(1)}, u32[]{:S(2)}, u32[]{:S(2)}) %collective-permute-start.1) | collective-permute-done | bytes 262176 | tf_op jit(solution)/shard_map/ppermute | solution.py:381
  74.6 0.7 placed.7
  (5 shorter events, 0.0 us)
Async XLA Ops:
  0.0 20.4 %copy-start = (f32[1,16,4096]{2,1,0:T(8,128)S(1)}, f32[1,16,4096]{2,1,0:T(8,128)}, u32[]{:S(2)}) copy-start(f32[1,16,4096]{2,1,0:T(8,128)} %refs_2_.3) | copy-start | bytes 786436
  0.0 7.8 %copy-start.2 = (f32[1,3,3,4096]{3,0,2,1:T(1,128)S(1)}, f32[1,3,3,4096]{3,0,2,1:T(1,128)}, u32[]{:S(2)}) copy-start(f32[1,3,3,4096]{3,0,2,1:T(1,128)} %param.6) | copy-start | bytes 442372
  0.0 20.4 %copy-start.3 = (f32[1,16,4096]{2,1,0:T(8,128)S(1)}, f32[1,16,4096]{2,1,0:T(8,128)}, u32[]{:S(2)}) copy-start(f32[1,16,4096]{2,1,0:T(8,128)} %param.8) | copy-start | bytes 786436
  1.1 6.7 %collective-permute-start = (bf16[1,3,2,4096]{3,2,1,0:T(2,128)(2,1)S(1)}, bf16[1,3,2,4096]{3,2,1,0:T(2,128)(2,1)S(1)}, u32[]{:S(2)}, u32[]{:S(2)}) collective-permute-start(bf16[1,3,2,4096]{3,2,1,0:T(2,128)(2,1)S(1)} %slice.3), channel_id=1, source_target_pairs={{0,32},{32,64},{64,96},{96,128},{128,160},{160,192},{192,224},{224... | collective-permute-start | bytes 147464 | tf_op jit(solution)/shard_map/ppermute | solution.py:285
  8.6 20.5 %all-to-all-start = ((bf16[16,32,128]{2,1,0:T(8,128)(2,1)}), bf16[16,32,128]{2,1,0:T(8,128)(2,1)S(1)}, u32[]{:S(2)}, u32[]{:S(2)}) async-start(bf16[16,32,128]{2,1,0:T(8,128)(2,1)} %get-tuple-element.35), calls=%async_computation | async-start | bytes 262144 | tf_op jit(solution)/shard_map/all_to_all | solution.py:282
  24.0 18.0 %copy-start.1 = (f32[1,16,4096]{2,1,0:T(8,128)S(1)}, f32[1,16,4096]{2,1,0:T(8,128)}, u32[]{:S(2)}) copy-start(f32[1,16,4096]{2,1,0:T(8,128)} %refs_2_.3) | copy-start | bytes 786436
  29.9 12.2 %all-to-all-start.1 = ((bf16[16,32,128]{2,1,0:T(8,128)(2,1)}), bf16[16,32,128]{2,1,0:T(8,128)(2,1)S(1)}, u32[]{:S(2)}, u32[]{:S(2)}) async-start(bf16[16,32,128]{2,1,0:T(8,128)(2,1)} %scan_chunks.1), calls=%async_computation.1 | async-start | bytes 262144 | tf_op jit(solution)/shard_map/all_to_all | solution.py:282
  43.8 19.7 %collective-permute-start.4 = (bf16[1,128,1024]{2,1,0:T(8,128)(2,1)S(1)}, bf16[1,128,1024]{2,1,0:T(8,128)(2,1)S(1)}, u32[]{:S(2)}, u32[]{:S(2)}) collective-permute-start(bf16[1,128,1024]{2,1,0:T(8,128)(2,1)S(1)} %finished.3), channel_id=1, source_target_pairs={{0,1},{1,2},{2,3},{3,4},{4,5},{5,6},{6,7},{7,8},{8,9},{9,10},{10,1... | collective-permute-start | bytes 786440 | tf_op jit(solution)/shard_map/ppermute | solution.py:381
  49.0 15.3 %collective-permute-start.3 = (bf16[1,128,1024]{2,1,0:T(8,128)(2,1)S(1)}, bf16[1,128,1024]{2,1,0:T(8,128)(2,1)S(1)}, u32[]{:S(2)}, u32[]{:S(2)}) collective-permute-start(bf16[1,128,1024]{2,1,0:T(8,128)(2,1)S(1)} %finished.2), channel_id=1, source_target_pairs={{0,1},{1,2},{2,3},{3,4},{4,5},{5,6},{6,7},{7,8},{8,9},{9,10},{10,1... | collective-permute-start | bytes 786440 | tf_op jit(solution)/shard_map/ppermute | solution.py:381
  55.2 14.2 %collective-permute-start.2 = (bf16[1,128,1024]{2,1,0:T(8,128)(2,1)S(1)}, bf16[1,128,1024]{2,1,0:T(8,128)(2,1)S(1)}, u32[]{:S(2)}, u32[]{:S(2)}) collective-permute-start(bf16[1,128,1024]{2,1,0:T(8,128)(2,1)S(1)} %mixed_output.3), channel_id=1, source_target_pairs={{0,1},{1,2},{2,3},{3,4},{4,5},{5,6},{6,7},{7,8},{8,9},{9,10},{10,1... | collective-permute-start | bytes 786440 | tf_op jit(solution)/shard_map/ppermute | solution.py:381
  61.0 13.6 %collective-permute-start.1 = (bf16[1,128,1024]{2,1,0:T(8,128)(2,1)S(1)}, bf16[1,128,1024]{2,1,0:T(8,128)(2,1)S(1)}, u32[]{:S(2)}, u32[]{:S(2)}) collective-permute-start(bf16[1,128,1024]{2,1,0:T(8,128)(2,1)S(1)} %mixed_output.2), channel_id=1, source_target_pairs={{0,1},{1,2},{2,3},{3,4},{4,5},{5,6},{6,7},{7,8},{8,9},{9,10},{10,1... | collective-permute-start | bytes 786440 | tf_op jit(solution)/shard_map/ppermute | solution.py:381

commit v5 on v4

--- a/solution.py
+++ b/solution.py
@@ -12,7 +12,9 @@
 ROWS = 8
 GROUP = ROWS * LANES
 EARLY = 2
+FIRST_OPS = 25600
 PLACE_OPS = 10000
+UNPACK = 0
 PIECES = 4
 f32 = jnp.float32
 bf16 = jnp.bfloat16
@@ -161,13 +163,78 @@
     lax.fori_loop(1, length // 2, step, states, unroll=3)
 
 
+def pack_kernel(order, length, pitch, total, inputs, taps, gate, edge, rates, scaled, skip, packed, raw, mode_rows):
+    rate_list = by_mode(mode_rows, rates[0], order)
+    tiles = []
+    for rate in rate_list:
+        for _ in range(3):
+            term = rate.astype(bf16).astype(f32)
+            tiles.append(term)
+            rate = rate - term
+    for m in range(0, len(tiles), 2):
+        packed[0, length + m // 2] = jnp.concatenate(tiles[m : m + 2], axis=0).astype(bf16)
+    steps = [jnp.exp(-(rate / total)) for rate in rate_list]
+    scales = by_mode(mode_rows, scaled[...], order)
+    weights = [taps[a] for a in range(TAPS)]
+    for k in range(ROWS):
+        raw[pl.ds(k * pitch, length), :] = inputs[0, 0, :, k * LANES : (k + 1) * LANES].astype(f32)
+
+    def lead_step(pair, before):
+        leads = []
+        for sub in range(2):
+            one, two = before
+            now = raw[pl.ds(2 * pair + sub, ROWS, stride=pitch), :]
+            leads.append(weights[0] * now + weights[1] * one + weights[2] * two)
+            before = (now, one)
+        packed[0, pair] = jnp.concatenate(leads, axis=0).astype(bf16)
+        return before
+
+    lax.fori_loop(0, length // 2, lead_step, (edge[1], edge[0]), unroll=4)
+
+    def tokens(pair, states, both):
+        mixes = []
+        for gated in both:
+            states = tuple(s * x + gated for s, x in zip(steps, states))
+            mixes.append(tree_sum([w * x for w, x in zip(scales, states)]) + skip[...] * gated)
+        packed[0, length // 2 + pair] = jnp.concatenate(mixes, axis=0).astype(bf16)
+        return states
+
+    def step(pair, states):
+        both = gate[0, pair].astype(f32)
+        return tokens(pair, states, (both[:ROWS], both[ROWS:]))
+
+    states = tokens(0, (jnp.zeros((ROWS, LANES), f32),) * order, (edge[2], edge[3]))
+    lax.fori_loop(1, length // 2, step, states, unroll=3)
+
+
+def unpack_kernel(order, length, pitch, total, packed, start, *rest):
+    out_ref, rows = rest[-2:]
+    tiles = []
+    for m in range(0, 3 * order, 2):
+        both = packed[0, length + m // 2].astype(f32)
+        tiles += [both[:ROWS], both[ROWS:]]
+    steps = [jnp.exp(-((tiles[3 * n] + tiles[3 * n + 1] + tiles[3 * n + 2]) / total)) for n in range(order)]
+
+    def step(pair, terms):
+        lead, mix = packed[0, pair].astype(f32), packed[0, length // 2 + pair].astype(f32)
+        for sub in range(2):
+            part = slice(sub * ROWS, (sub + 1) * ROWS)
+            terms = tuple(s * x for s, x in zip(steps, terms))
+            rows[pl.ds(2 * pair + sub, ROWS, stride=pitch), :] = lead[part] * (mix[part] + tree_sum(list(terms)))
+        return terms
+
+    lax.fori_loop(0, length // 2, step, tuple(start[n] for n in range(order)), unroll=4)
+    for k in range(ROWS):
+        out_ref[0, :, pl.ds(k * LANES, LANES)] = rows[pl.ds(k * pitch, length), :].astype(bf16)
+
+
 def finish_kernel(order, length, pitch, total, first, count, *refs):
     sources, (rates, scaled, start, out_ref, parts, rows, mode_rows, sems) = refs[: 2 * count], refs[2 * count :]
     piece = length // PIECES
 
     def fetch(g, i, c):
         which, at = 2 * g + i, pl.ds(c * piece, piece)
-        return pltpu.make_async_copy(sources[which].at[0, at], parts.at[which, at], sems.at[which, c])
+        return pltpu.make_async_copy(sources[which].at[first, at], parts.at[which, at], sems.at[which, c])
 
     for g in range(count):
         for c in range(PIECES):
@@ -322,19 +389,33 @@
 
     def local_mix(at, gated):
         return call(
-            functools.partial(mix_kernel, order, length, pitch, total), "local_mix", 1, 80, length,
+            functools.partial(mix_kernel, order, length, pitch, total), "local_mix", EARLY, 80, length,
             [pl.BlockSpec((1, 1, length, GROUP), lambda g: (0, 0, 0, at + g)), stack(TAPS, at),
              pairs(at), stack(4, at), rate_block(at), scale_block(at),
              pl.BlockSpec((ROWS, LANES), lambda g: (at + g, 0))],
-            [tokens(0), tokens(0)], [pltpu.HBM((1, length, ROWS, LANES), f32)] * 2,
+            [tokens(0), tokens(0)], [pltpu.HBM((EARLY, length, ROWS, LANES), f32)] * 2,
             [pltpu.VMEM((ROWS * pitch, LANES), f32), mode_rows],
         )(held(projected), held(taps), gated, edge, held(decay_rate), scaled, held(skip))
 
+    def packed_group(at, gated):
+        return call(
+            functools.partial(pack_kernel, order, length, pitch, total), "packed", 1, 80, length,
+            [pl.BlockSpec((1, 1, length, GROUP), lambda g: (0, 0, 0, at)), stack(TAPS, at),
+             pairs(at), stack(4, at), rate_block(at), scale_block(at),
+             pl.BlockSpec((ROWS, LANES), lambda g: (at, 0))],
+            pl.BlockSpec((1, packed_rows, 2 * ROWS, LANES), lambda g: (0, 0, 0, 0)),
+            pltpu.HBM((1, packed_rows, 2 * ROWS, LANES), bf16),
+            [pltpu.VMEM((ROWS * pitch, LANES), f32), mode_rows],
+        )(held(projected), held(taps), gated, edge, held(decay_rate), scaled, held(skip))
+
+    last = groups - 1
+    packed_rows = length + 3 * order // 2
     wire, gate, residue = after(wire, gate, residue)
     scaled = residue[0] * jnp.sqrt(-jnp.expm1(-2.0 * (decay_rate[0] / total)))
     came = to_all(wire)
-    mixes = [local_mix(0, gate)]
-    came, mixes, gate = after(came, mixes, gate)
+    packed = packed_group(last, gate)
+    packed_before = lax.ppermute(packed, "pipe", onward)
+    came, packed, gate, scaled = after(came, packed, gate, scaled)
     enter = pl.pallas_call(
         scan_kernel,
         out_shape=jax.ShapeDtypeStruct(came.shape, bf16),
@@ -343,12 +424,15 @@
     )(came, span)
     enter, gate = after(enter, gate)
     start = to_all(enter)
-    mixes.append(local_mix(1, gate))
+    mixes = local_mix(0, gate)
     start, mixes, gate = after(start, mixes, gate)
+    scale_tile = scaled[:, last * GROUP :].reshape(order, ROWS, LANES)
+    sent = (start[:, last * ROWS :].astype(f32) * scale_tile).astype(bf16)
+    start_before = lax.ppermute(sent, "pipe", onward).astype(f32)
     in_vmem = pl.BlockSpec(memory_space=pltpu.VMEM)
     share = jax.ShapeDtypeStruct((1, length, GROUP), bf16)
     handed = None
-    for at in range(groups):
+    for at in range(last):
         if at < EARLY:
             output = pl.pallas_call(
                 functools.partial(finish_kernel, order, length, pitch, total, at, 1),
@@ -363,10 +447,10 @@
                 ],
                 compiler_params=pltpu.CompilerParams(vmem_limit_bytes=16 << 20),
                 cost_estimate=pl.CostEstimate(
-                    flops=40 * length * GROUP, bytes_accessed=8 * length * GROUP, transcendentals=0
+                    flops=(40 if at else FIRST_OPS) * length * GROUP, bytes_accessed=8 * length * GROUP, transcendentals=0
                 ),
                 name="finished",
-            )(*map(held, mixes[at]), decay_rate, scaled, start)
+            )(*map(held, mixes), decay_rate, scaled, start)
         else:
             output = call(
                 functools.partial(whole_kernel, order, length, pitch, total, at % 2), "mixed_output", 1, 90, length,
@@ -378,12 +462,21 @@
                 [pltpu.VMEM((ROWS * pitch, LANES), f32)] * 2
                 + [mode_rows, pltpu.VMEM((order, 2 * ROWS, LANES), f32)],
             )(held(projected), held(taps), gate, edge, held(decay_rate), scaled, held(skip), start)
+        if at == 0:
+            output, packed_before = after(output, packed_before)
         came = lax.ppermute(output, "pipe", onward)
         given = [came] if handed is None else [came, handed]
         handed = call(
             place_kernel, "placed", 1, PLACE_OPS, length, [out_block(0)] + [anywhere] * (len(given) - 1),
             out_block(at), jax.ShapeDtypeStruct((1, length, width), bf16), [], {1: 0} if len(given) > 1 else {},
         )(*given)
+        if at == UNPACK:
+            handed = call(
+                functools.partial(unpack_kernel, order, length, pitch, total), "finished_ahead", 1, PLACE_OPS, length,
+                [pl.BlockSpec((1, packed_rows, 2 * ROWS, LANES), lambda g: (0, 0, 0, 0)), stack(order, 0), anywhere],
+                out_block(last), jax.ShapeDtypeStruct((1, length, width), bf16),
+                [pltpu.VMEM((ROWS * pitch, LANES), f32)], {2: 0},
+            )(packed_before, start_before, handed)
     return handed
 
 

time: 75.9 us -> 75.3 us (level)
  the two profiles are of different devices: /device:TPU:32 before, /device:TPU:24 now
where the time goes in v5:
time: 75.3 us; the launch traced here: 74.7 us
  starting transfers between devices  37.2 us (49%)
  Pallas kernels  24.9 us (33%)
  waiting for transfers between devices  11.1 us (15%)
  local copies, waits for them, and re-layouts  1.09 us (1%)
    all_to_all x2, starting transfers between devices, shards(): to_all = lambda x: lax.all_to_all(x, 'seq', 0, 0, tiled=True)  17.4 us
    ppermute x3, starting transfers between devices, shards(): came = lax.ppermute(output, 'pipe', onward)  11.4 us
    ppermute x3, waiting for transfers between devices, shards(): came = lax.ppermute(output, 'pipe', onward)  5.86 us
    all_to_all x2, waiting for transfers between devices, shards(): to_all = lambda x: lax.all_to_all(x, 'seq', 0, 0, tiled=True)  5.25 us
    pallas_call x1, Pallas kernels, local_mix(): call(functools.partial(mix_kernel, order, length, pitch, total), 'local_m...  5.05 us
    pallas_call x1, Pallas kernels, shards(): pl.pallas_call(functools.partial(state_kernel, order, length, pitch, tota...  4.96 us
    pallas_call x2, Pallas kernels, shards(): pl.pallas_call(functools.partial(finish_kernel, order, length, pitch, tot...  3.54 us
    ppermute x1, starting transfers between devices, shards(): packed_before = lax.ppermute(packed, 'pipe', onward)  3.52 us
  transfers between devices with their start and end apart: 8, of which 3 were waited for; matrix products, arithmetic and copies ran while one was open for 0% of the time, Pallas kernels for 31%

profile of v5, /device:TPU:24, one launch (start us, length us, event | category | flops | bytes accessed | tf_op | source)
XLA Modules:
  0.0 74.7 jit_solution(7677001885678712146)
XLA Ops:
  0.0 1.0 %slice.9 = bf16[1,3,2,4096]{3,2,1,0:T(2,128)(2,1)S(1)} slice(bf16[1,3,128,4096]{3,2,1,0:T(8,128)(2,1)} %inputs.7), slice={[0:1], [0:3], [126:128], [0:4096]} | slice | bytes 98304 | tf_op jit(solution)/shard_map/slice | solution.py:352
  1.1 1.7 %collective-permute-start = (bf16[1,3,2,4096]{3,2,1,0:T(2,128)(2,1)S(1)}, bf16[1,3,2,4096]{3,2,1,0:T(2,128)(2,1)S(1)}, u32[]{:S(2)}, u32[]{:S(2)}) collective-permute-start(bf16[1,3,2,4096]{3,2,1,0:T(2,128)(2,1)S(1)} %slice.9), channel_id=1, source_target_pairs={{0,32},{32,64},{64,96},{96,128},{128,160},{160,192},{192,224},{224... | collective-permute-start | bytes 147464 | tf_op jit(solution)/shard_map/ppermute | solution.py:352
  2.8 5.0 %local_states.1 = (f32[16,32,128]{2,1,0:T(8,128)S(1)}, f32[16,32,128]{2,1,0:T(8,128)S(1)}, f32[4,32,128]{2,1,0:T(8,128)S(1)}, bf16[4,64,16,128]{3,2,1,0:T(8,128)(2,1)S(1)}) custom-call(bf16[1,3,128,4096]{3,2,1,0:T(8,128)(2,1)} %inputs.7, f32[9,32,128]{2,1,0:T(8,128)} %bitcast.10, f32[1,16,4096]{2,1,0:T(8,128)} %refs_2_.3), custom_call_target="tpu_custom_call" | custom-call | flops 28835840 | bytes 4194304 | tf_op jit(solution)/shard_map/local_states/pallas_call | solution.py:363
  7.8 0.0 collective-permute-done.rim
  7.8 0.8 %first_tokens.1 = (bf16[16,32,128]{2,1,0:T(8,128)(2,1)}, f32[4,32,128]{2,1,0:T(8,128)S(1)}) custom-call(bf16[1,3,2,4096]{3,2,1,0:T(2,128)(2,1)S(1)} %collective-permute-done.rim, f32[4,32,128]{2,1,0:T(8,128)S(1)} %get-tuple-element.27.head, f32[9,32,128]{2,1,0:T(8,128)S(1)} %bitcast.14, f32[16,32,128]{2,1,0:T(8,128)S(1)} %get-tuple-element.28.ends, ...), custom_call_target="tpu_custom_call" | custom-call | tf_op jit(solution)/shard_map/first_tokens/pallas_call | solution.py:382
  8.6 11.8 %all-to-all-start = ((bf16[16,32,128]{2,1,0:T(8,128)(2,1)}), bf16[16,32,128]{2,1,0:T(8,128)(2,1)S(1)}, u32[]{:S(2)}, u32[]{:S(2)}) async-start(bf16[16,32,128]{2,1,0:T(8,128)(2,1)} %get-tuple-element.32), calls=%async_computation | async-start | bytes 262144 | tf_op jit(solution)/shard_map/all_to_all | solution.py:349
  20.4 0.0 copy-done
  20.4 0.0 copy-done.3
  20.4 0.2 multiply_bitcast_fusion.scaled.refs_3_
  20.6 3.5 %packed.1 = bf16[1,152,16,128]{3,2,1,0:T(8,128)(2,1)} custom-call(bf16[1,3,128,4096]{3,2,1,0:T(8,128)(2,1)} %inputs.7, f32[9,32,128]{2,1,0:T(8,128)} %bitcast.11, bf16[4,64,16,128]{3,2,1,0:T(8,128)(2,1)S(1)} %get-tuple-element.43.gate, f32[4,32,128]{2,1,0:T(8,128)S(1)} %get-tuple-element.34.edge, f32[1,16,4096]{2,1,0:T(8,128)} %refs_2_.3, ...), custom_call_target="tpu_custom_call" | custom-call | flops 10485760 | bytes 1048576 | tf_op jit(solution)/shard_map/packed/pallas_call | solution.py:401
  24.1 3.5 %collective-permute-start.3 = (bf16[1,152,16,128]{3,2,1,0:T(8,128)(2,1)}, bf16[1,152,16,128]{3,2,1,0:T(8,128)(2,1)S(1)}, u32[]{:S(2)}, u32[]{:S(2)}) collective-permute-start(bf16[1,152,16,128]{3,2,1,0:T(8,128)(2,1)} %packed.1), channel_id=1, source_target_pairs={{0,1},{1,2},{2,3},{3,4},{4,5},{5,6},{6,7},{7,8},{8,9},{9,10},{10,1... | collective-permute-start | bytes 1867784 | tf_op jit(solution)/shard_map/ppermute | solution.py:417
  27.6 1.6 %all-to-all-done.came = bf16[16,32,128]{2,1,0:T(8,128)(2,1)S(1)} async-done(((bf16[16,32,128]{2,1,0:T(8,128)(2,1)}), bf16[16,32,128]{2,1,0:T(8,128)(2,1)S(1)}, u32[]{:S(2)}, u32[]{:S(2)}) %all-to-all-start) | async-done | bytes 131104 | tf_op jit(solution)/shard_map/all_to_all | solution.py:349
  29.2 0.7 scan_chunks.1
  29.9 5.7 %all-to-all-start.1 = ((bf16[16,32,128]{2,1,0:T(8,128)(2,1)}), bf16[16,32,128]{2,1,0:T(8,128)(2,1)S(1)}, u32[]{:S(2)}, u32[]{:S(2)}) async-start(bf16[16,32,128]{2,1,0:T(8,128)(2,1)} %scan_chunks.1), calls=%async_computation.1 | async-start | bytes 262144 | tf_op jit(solution)/shard_map/all_to_all | solution.py:349
  35.6 5.1 %local_mix.1 = (f32[2,128,8,128]{3,2,1,0:T(8,128)}, f32[2,128,8,128]{3,2,1,0:T(8,128)}) custom-call(bf16[1,3,128,4096]{3,2,1,0:T(8,128)(2,1)} %inputs.7, f32[9,32,128]{2,1,0:T(8,128)} %bitcast.12, bf16[4,64,16,128]{3,2,1,0:T(8,128)(2,1)S(1)} %get-tuple-element.43.gate, f32[4,32,128]{2,1,0:T(8,128)S(1)} %get-tuple-element.34.edge, f32[1,16,4096]{2,1,0:T(8,128)} %refs_2_.3, ...), custom_call_target="tpu_custom_call" | custom-call | flops 20971520 | bytes 2097152 | tf_op jit(solution)/shard_map/local_mix/pallas_call | solution.py:391
  40.6 3.7 %all-to-all-done.1.start.refs_4_ = bf16[16,32,128]{2,1,0:T(8,128)(2,1)S(1)} async-done(((bf16[16,32,128]{2,1,0:T(8,128)(2,1)}), bf16[16,32,128]{2,1,0:T(8,128)(2,1)S(1)}, u32[]{:S(2)}, u32[]{:S(2)}) %all-to-all-start.1) | async-done | bytes 131104 | tf_op jit(solution)/shard_map/all_to_all | solution.py:349
  44.3 1.8 %finished.3 = bf16[1,128,1024]{2,1,0:T(8,128)(2,1)S(1)} custom-call(f32[2,128,8,128]{3,2,1,0:T(8,128)} %get-tuple-element.45.refs_0_, f32[2,128,8,128]{3,2,1,0:T(8,128)} %get-tuple-element.46.refs_1_, f32[1,16,4096]{2,1,0:T(8,128)S(1)} %copy-done.1, f32[16,4096]{1,0:T(8,128)S(1)} %multiply_bitcast_fusion.scaled.refs_3_, ...), custom_call_target="tpu_custom_call" | custom-call | flops 3355443200 | bytes 1048576 | tf_op jit(solution)/shard_map/finished/pallas_call | solution.py:437
  46.1 0.0 collective-permute-done.3.packed
  46.1 3.4 %collective-permute-start.5 = (bf16[1,128,1024]{2,1,0:T(8,128)(2,1)S(1)}, bf16[1,128,1024]{2,1,0:T(8,128)(2,1)S(1)}, u32[]{:S(2)}, u32[]{:S(2)}) collective-permute-start(bf16[1,128,1024]{2,1,0:T(8,128)(2,1)S(1)} %finished.3), channel_id=1, source_target_pairs={{0,1},{1,2},{2,3},{3,4},{4,5},{5,6},{6,7},{7,8},{8,9},{9,10},{10,1... | collective-permute-start | bytes 786440 | tf_op jit(solution)/shard_map/ppermute | solution.py:467
  49.5 3.1 %collective-permute-start.4 = (bf16[16,8,128]{2,1,0:T(8,128)(2,1)S(1)}, bf16[16,8,128]{2,1,0:T(8,128)(2,1)S(1)}, u32[]{:S(2)}, u32[]{:S(2)}) collective-permute-start(bf16[16,8,128]{2,1,0:T(8,128)(2,1)S(1)} %fusion), channel_id=1, source_target_pairs={{0,1},{1,2},{2,3},{3,4},{4,5},{5,6},{6,7},{7,8},{8,9},{9,10},{10,1... | collective-permute-start | bytes 98312 | tf_op jit(solution)/shard_map/ppermute | solution.py:431
  52.7 1.8 %finished.2 = bf16[1,128,1024]{2,1,0:T(8,128)(2,1)S(1)} custom-call(f32[2,128,8,128]{3,2,1,0:T(8,128)} %get-tuple-element.45.refs_0_, f32[2,128,8,128]{3,2,1,0:T(8,128)} %get-tuple-element.46.refs_1_, f32[1,16,4096]{2,1,0:T(8,128)S(1)} %copy-done.1, f32[16,4096]{1,0:T(8,128)S(1)} %multiply_bitcast_fusion.scaled.refs_3_, ...), custom_call_target="tpu_custom_call" | custom-call | flops 5242880 | bytes 1048576 | tf_op jit(solution)/shard_map/finished/pallas_call | solution.py:437
  54.4 4.6 %collective-permute-start.2 = (bf16[1,128,1024]{2,1,0:T(8,128)(2,1)S(1)}, bf16[1,128,1024]{2,1,0:T(8,128)(2,1)S(1)}, u32[]{:S(2)}, u32[]{:S(2)}) collective-permute-start(bf16[1,128,1024]{2,1,0:T(8,128)(2,1)S(1)} %finished.2), channel_id=1, source_target_pairs={{0,1},{1,2},{2,3},{3,4},{4,5},{5,6},{6,7},{7,8},{8,9},{9,10},{10,1... | collective-permute-start | bytes 786440 | tf_op jit(solution)/shard_map/ppermute | solution.py:467
  59.1 2.7 %mixed_output.1 = bf16[1,128,1024]{2,1,0:T(8,128)(2,1)S(1)} custom-call(bf16[1,3,128,4096]{3,2,1,0:T(8,128)(2,1)} %inputs.7, f32[9,32,128]{2,1,0:T(8,128)} %bitcast.13, bf16[4,64,16,128]{3,2,1,0:T(8,128)(2,1)S(1)} %get-tuple-element.43.gate, f32[4,32,128]{2,1,0:T(8,128)S(1)} %get-tuple-element.34.edge, f32[1,16,4096]{2,1,0:T(8,128)} %refs_2_.3, ...), custom_call_target="tpu_custom_call" | custom-call | flops 11796480 | bytes 1048576 | tf_op jit(solution)/shard_map/mixed_output/pallas_call | solution.py:455
  61.8 3.4 %collective-permute-start.1 = (bf16[1,128,1024]{2,1,0:T(8,128)(2,1)S(1)}, bf16[1,128,1024]{2,1,0:T(8,128)(2,1)S(1)}, u32[]{:S(2)}, u32[]{:S(2)}) collective-permute-start(bf16[1,128,1024]{2,1,0:T(8,128)(2,1)S(1)} %mixed_output.1), channel_id=1, source_target_pairs={{0,1},{1,2},{2,3},{3,4},{4,5},{5,6},{6,7},{7,8},{8,9},{9,10},{10,1... | collective-permute-start | bytes 786440 | tf_op jit(solution)/shard_map/ppermute | solution.py:467
  65.2 0.0 collective-permute-done.4
  65.3 0.0 collective-permute-done.5.part
  65.3 0.7 placed.3.rest_0_
  66.0 1.5 %finished_ahead.1.rest_0_ = bf16[1,128,4096]{2,1,0:T(8,128)(2,1)} custom-call(bf16[1,152,16,128]{3,2,1,0:T(8,128)(2,1)S(1)} %collective-permute-done.3.packed, f32[16,8,128]{2,1,0:T(8,128)S(1)} %convert_element_type.11.start, bf16[1,128,4096]{2,1,0:T(8,128)(2,1)} %placed.3.rest_0_), custom_call_target="tpu_custom_call", output_to_operand_aliasing={{}: (2, {})} | custom-call | flops 1310720000 | bytes 1048576 | tf_op jit(solution)/shard_map/finished_ahead/pallas_call | solution.py:474
  67.4 0.0 collective-permute-done.2.part
  67.4 0.7 placed.4.rest_0_
  68.2 5.9 %collective-permute-done.1.part = bf16[1,128,1024]{2,1,0:T(8,128)(2,1)S(1)} collective-permute-done((bf16[1,128,1024]{2,1,0:T(8,128)(2,1)S(1)}, bf16[1,128,1024]{2,1,0:T(8,128)(2,1)S(1)}, u32[]{:S(2)}, u32[]{:S(2)}) %collective-permute-start.1) | collective-permute-done | bytes 262176 | tf_op jit(solution)/shard_map/ppermute | solution.py:467
  74.0 0.7 placed.5
  (10 shorter events, 0.1 us)
Async XLA Ops:
  0.0 7.8 %copy-start.2 = (f32[1,3,3,4096]{3,0,2,1:T(1,128)S(1)}, f32[1,3,3,4096]{3,0,2,1:T(1,128)}, u32[]{:S(2)}) copy-start(f32[1,3,3,4096]{3,0,2,1:T(1,128)} %param.6) | copy-start | bytes 442372
  0.0 20.4 %copy-start = (f32[1,16,4096]{2,1,0:T(8,128)S(1)}, f32[1,16,4096]{2,1,0:T(8,128)}, u32[]{:S(2)}) copy-start(f32[1,16,4096]{2,1,0:T(8,128)} %refs_2_.3) | copy-start | bytes 786436
  0.0 20.4 %copy-start.3 = (f32[1,16,4096]{2,1,0:T(8,128)S(1)}, f32[1,16,4096]{2,1,0:T(8,128)}, u32[]{:S(2)}) copy-start(f32[1,16,4096]{2,1,0:T(8,128)} %param.8) | copy-start | bytes 786436
  1.1 6.7 %collective-permute-start = (bf16[1,3,2,4096]{3,2,1,0:T(2,128)(2,1)S(1)}, bf16[1,3,2,4096]{3,2,1,0:T(2,128)(2,1)S(1)}, u32[]{:S(2)}, u32[]{:S(2)}) collective-permute-start(bf16[1,3,2,4096]{3,2,1,0:T(2,128)(2,1)S(1)} %slice.9), channel_id=1, source_target_pairs={{0,32},{32,64},{64,96},{96,128},{128,160},{160,192},{192,224},{224... | collective-permute-start | bytes 147464 | tf_op jit(solution)/shard_map/ppermute | solution.py:352
  8.6 20.5 %all-to-all-start = ((bf16[16,32,128]{2,1,0:T(8,128)(2,1)}), bf16[16,32,128]{2,1,0:T(8,128)(2,1)S(1)}, u32[]{:S(2)}, u32[]{:S(2)}) async-start(bf16[16,32,128]{2,1,0:T(8,128)(2,1)} %get-tuple-element.32), calls=%async_computation | async-start | bytes 262144 | tf_op jit(solution)/shard_map/all_to_all | solution.py:349
  24.1 20.2 %copy-start.1 = (f32[1,16,4096]{2,1,0:T(8,128)S(1)}, f32[1,16,4096]{2,1,0:T(8,128)}, u32[]{:S(2)}) copy-start(f32[1,16,4096]{2,1,0:T(8,128)} %refs_2_.3) | copy-start | bytes 786436
  24.1 22.0 %collective-permute-start.3 = (bf16[1,152,16,128]{3,2,1,0:T(8,128)(2,1)}, bf16[1,152,16,128]{3,2,1,0:T(8,128)(2,1)S(1)}, u32[]{:S(2)}, u32[]{:S(2)}) collective-permute-start(bf16[1,152,16,128]{3,2,1,0:T(8,128)(2,1)} %packed.1), channel_id=1, source_target_pairs={{0,1},{1,2},{2,3},{3,4},{4,5},{5,6},{6,7},{7,8},{8,9},{9,10},{10,1... | collective-permute-start | bytes 1867784 | tf_op jit(solution)/shard_map/ppermute | solution.py:417
  29.9 14.4 %all-to-all-start.1 = ((bf16[16,32,128]{2,1,0:T(8,128)(2,1)}), bf16[16,32,128]{2,1,0:T(8,128)(2,1)S(1)}, u32[]{:S(2)}, u32[]{:S(2)}) async-start(bf16[16,32,128]{2,1,0:T(8,128)(2,1)} %scan_chunks.1), calls=%async_computation.1 | async-start | bytes 262144 | tf_op jit(solution)/shard_map/all_to_all | solution.py:349
  46.1 19.2 %collective-permute-start.5 = (bf16[1,128,1024]{2,1,0:T(8,128)(2,1)S(1)}, bf16[1,128,1024]{2,1,0:T(8,128)(2,1)S(1)}, u32[]{:S(2)}, u32[]{:S(2)}) collective-permute-start(bf16[1,128,1024]{2,1,0:T(8,128)(2,1)S(1)} %finished.3), channel_id=1, source_target_pairs={{0,1},{1,2},{2,3},{3,4},{4,5},{5,6},{6,7},{7,8},{8,9},{9,10},{10,1... | collective-permute-start | bytes 786440 | tf_op jit(solution)/shard_map/ppermute | solution.py:467
  49.5 15.7 %collective-permute-start.4 = (bf16[16,8,128]{2,1,0:T(8,128)(2,1)S(1)}, bf16[16,8,128]{2,1,0:T(8,128)(2,1)S(1)}, u32[]{:S(2)}, u32[]{:S(2)}) collective-permute-start(bf16[16,8,128]{2,1,0:T(8,128)(2,1)S(1)} %fusion), channel_id=1, source_target_pairs={{0,1},{1,2},{2,3},{3,4},{4,5},{5,6},{6,7},{7,8},{8,9},{9,10},{10,1... | collective-permute-start | bytes 98312 | tf_op jit(solution)/shard_map/ppermute | solution.py:431
  54.4 13.0 %collective-permute-start.2 = (bf16[1,128,1024]{2,1,0:T(8,128)(2,1)S(1)}, bf16[1,128,1024]{2,1,0:T(8,128)(2,1)S(1)}, u32[]{:S(2)}, u32[]{:S(2)}) collective-permute-start(bf16[1,128,1024]{2,1,0:T(8,128)(2,1)S(1)} %finished.2), channel_id=1, source_target_pairs={{0,1},{1,2},{2,3},{3,4},{4,5},{5,6},{6,7},{7,8},{8,9},{9,10},{10,1... | collective-permute-start | bytes 786440 | tf_op jit(solution)/shard_map/ppermute | solution.py:467
  61.8 12.2 %collective-permute-start.1 = (bf16[1,128,1024]{2,1,0:T(8,128)(2,1)S(1)}, bf16[1,128,1024]{2,1,0:T(8,128)(2,1)S(1)}, u32[]{:S(2)}, u32[]{:S(2)}) collective-permute-start(bf16[1,128,1024]{2,1,0:T(8,128)(2,1)S(1)} %mixed_output.1), channel_id=1, source_target_pairs={{0,1},{1,2},{2,3},{3,4},{4,5},{5,6},{6,7},{7,8},{8,9},{9,10},{10,1... | collective-permute-start | bytes 786440 | tf_op jit(solution)/shard_map/ppermute | solution.py:467

commit v6 on v5

--- a/solution.py
+++ b/solution.py
@@ -14,7 +14,7 @@
 EARLY = 2
 FIRST_OPS = 25600
 PLACE_OPS = 10000
-UNPACK = 0
+UNPACK = 1
 PIECES = 4
 f32 = jnp.float32
 bf16 = jnp.bfloat16
@@ -343,7 +343,7 @@
     total = length * nseq
     groups = width // GROUP
     tiles = width // LANES
-    pitch = length + 8
+    pitch = length + 9
     onward = [(i, i + 1) for i in range(sections - 1)]
     held = lambda x: pltpu.with_memory_space_constraint(x, pltpu.HBM)
     to_all = lambda x: lax.all_to_all(x, "seq", 0, 0, tiled=True)

time: 75.3 us -> 74.8 us (level)
    ppermute x3, starting transfers between devices: 11.4 us -> 9.9 us  [shards(): came = lax.ppermute(output, 'pipe', onward)]
    ppermute x1, starting transfers between devices: 3.11 us -> 4.61 us  [shards(): start_before = lax.ppermute(sent, 'pipe', onward).astype(f32)]
  transfers between devices with their start and end apart: 8 -> 8, of which waited for: 3 -> 4; matrix products, arithmetic and copies ran while one was open for 0% -> 0% of each run, Pallas kernels for 31% -> 31%
where the time goes in v6:
time: 74.8 us; the launch traced here: 74.3 us
  starting transfers between devices  37.2 us (50%)
  Pallas kernels  24.4 us (33%)
  waiting for transfers between devices  11.3 us (15%)
  local copies, waits for them, and re-layouts  1.09 us (1%)
    all_to_all x2, starting transfers between devices, shards(): to_all = lambda x: lax.all_to_all(x, 'seq', 0, 0, tiled=True)  17.4 us
    ppermute x3, starting transfers between devices, shards(): came = lax.ppermute(output, 'pipe', onward)  9.9 us
    ppermute x3, waiting for transfers between devices, shards(): came = lax.ppermute(output, 'pipe', onward)  5.44 us
    all_to_all x2, waiting for transfers between devices, shards(): to_all = lambda x: lax.all_to_all(x, 'seq', 0, 0, tiled=True)  5.38 us
    pallas_call x1, Pallas kernels, local_mix(): call(functools.partial(mix_kernel, order, length, pitch, total), 'local_m...  4.98 us
    pallas_call x1, Pallas kernels, shards(): pl.pallas_call(functools.partial(state_kernel, order, length, pitch, tota...  4.78 us
    ppermute x1, starting transfers between devices, shards(): start_before = lax.ppermute(sent, 'pipe', onward).astype(f32)  4.61 us
    pallas_call x2, Pallas kernels, shards(): pl.pallas_call(functools.partial(finish_kernel, order, length, pitch, tot...  3.52 us
  transfers between devices with their start and end apart: 8, of which 4 were waited for; matrix products, arithmetic and copies ran while one was open for 0% of the time, Pallas kernels for 31%

profile of v6, /device:TPU:24, one launch (start us, length us, event | category | flops | bytes accessed | tf_op | source)
XLA Modules:
  0.0 74.3 jit_solution(6584546798358232488)
XLA Ops:
  0.0 1.0 %slice.9 = bf16[1,3,2,4096]{3,2,1,0:T(2,128)(2,1)S(1)} slice(bf16[1,3,128,4096]{3,2,1,0:T(8,128)(2,1)} %inputs.7), slice={[0:1], [0:3], [126:128], [0:4096]} | slice | bytes 98304 | tf_op jit(solution)/shard_map/slice | solution.py:352
  1.1 1.7 %collective-permute-start = (bf16[1,3,2,4096]{3,2,1,0:T(2,128)(2,1)S(1)}, bf16[1,3,2,4096]{3,2,1,0:T(2,128)(2,1)S(1)}, u32[]{:S(2)}, u32[]{:S(2)}) collective-permute-start(bf16[1,3,2,4096]{3,2,1,0:T(2,128)(2,1)S(1)} %slice.9), channel_id=1, source_target_pairs={{0,32},{32,64},{64,96},{96,128},{128,160},{160,192},{192,224},{224... | collective-permute-start | bytes 147464 | tf_op jit(solution)/shard_map/ppermute | solution.py:352
  2.8 4.8 %local_states.1 = (f32[16,32,128]{2,1,0:T(8,128)S(1)}, f32[16,32,128]{2,1,0:T(8,128)S(1)}, f32[4,32,128]{2,1,0:T(8,128)S(1)}, bf16[4,64,16,128]{3,2,1,0:T(8,128)(2,1)S(1)}) custom-call(bf16[1,3,128,4096]{3,2,1,0:T(8,128)(2,1)} %inputs.7, f32[9,32,128]{2,1,0:T(8,128)} %bitcast.10, f32[1,16,4096]{2,1,0:T(8,128)} %refs_2_.3), custom_call_target="tpu_custom_call" | custom-call | flops 28835840 | bytes 4194304 | tf_op jit(solution)/shard_map/local_states/pallas_call | solution.py:363
  7.6 0.0 collective-permute-done.rim
  7.6 0.0 copy-done.2
  7.6 0.8 %first_tokens.1 = (bf16[16,32,128]{2,1,0:T(8,128)(2,1)}, f32[4,32,128]{2,1,0:T(8,128)S(1)}) custom-call(bf16[1,3,2,4096]{3,2,1,0:T(2,128)(2,1)S(1)} %collective-permute-done.rim, f32[4,32,128]{2,1,0:T(8,128)S(1)} %get-tuple-element.27.head, f32[9,32,128]{2,1,0:T(8,128)S(1)} %bitcast.14, f32[16,32,128]{2,1,0:T(8,128)S(1)} %get-tuple-element.28.ends, ...), custom_call_target="tpu_custom_call" | custom-call | tf_op jit(solution)/shard_map/first_tokens/pallas_call | solution.py:382
  8.5 11.8 %all-to-all-start = ((bf16[16,32,128]{2,1,0:T(8,128)(2,1)}), bf16[16,32,128]{2,1,0:T(8,128)(2,1)S(1)}, u32[]{:S(2)}, u32[]{:S(2)}) async-start(bf16[16,32,128]{2,1,0:T(8,128)(2,1)} %get-tuple-element.32), calls=%async_computation | async-start | bytes 262144 | tf_op jit(solution)/shard_map/all_to_all | solution.py:349
  20.2 0.0 copy-done
  20.3 0.2 multiply_bitcast_fusion.scaled.refs_3_
  20.4 3.4 %packed.1 = bf16[1,152,16,128]{3,2,1,0:T(8,128)(2,1)} custom-call(bf16[1,3,128,4096]{3,2,1,0:T(8,128)(2,1)} %inputs.7, f32[9,32,128]{2,1,0:T(8,128)} %bitcast.11, bf16[4,64,16,128]{3,2,1,0:T(8,128)(2,1)S(1)} %get-tuple-element.43.gate, f32[4,32,128]{2,1,0:T(8,128)S(1)} %get-tuple-element.34.edge, f32[1,16,4096]{2,1,0:T(8,128)} %refs_2_.3, ...), custom_call_target="tpu_custom_call" | custom-call | flops 10485760 | bytes 1048576 | tf_op jit(solution)/shard_map/packed/pallas_call | solution.py:401
  23.8 3.5 %collective-permute-start.2 = (bf16[1,152,16,128]{3,2,1,0:T(8,128)(2,1)}, bf16[1,152,16,128]{3,2,1,0:T(8,128)(2,1)S(1)}, u32[]{:S(2)}, u32[]{:S(2)}) collective-permute-start(bf16[1,152,16,128]{3,2,1,0:T(8,128)(2,1)} %packed.1), channel_id=1, source_target_pairs={{0,1},{1,2},{2,3},{3,4},{4,5},{5,6},{6,7},{7,8},{8,9},{9,10},{10,1... | collective-permute-start | bytes 1867784 | tf_op jit(solution)/shard_map/ppermute | solution.py:417
  27.4 1.6 %all-to-all-done.came = bf16[16,32,128]{2,1,0:T(8,128)(2,1)S(1)} async-done(((bf16[16,32,128]{2,1,0:T(8,128)(2,1)}), bf16[16,32,128]{2,1,0:T(8,128)(2,1)S(1)}, u32[]{:S(2)}, u32[]{:S(2)}) %all-to-all-start) | async-done | bytes 131104 | tf_op jit(solution)/shard_map/all_to_all | solution.py:349
  29.0 0.7 scan_chunks.1
  29.7 5.6 %all-to-all-start.1 = ((bf16[16,32,128]{2,1,0:T(8,128)(2,1)}), bf16[16,32,128]{2,1,0:T(8,128)(2,1)S(1)}, u32[]{:S(2)}, u32[]{:S(2)}) async-start(bf16[16,32,128]{2,1,0:T(8,128)(2,1)} %scan_chunks.1), calls=%async_computation.1 | async-start | bytes 262144 | tf_op jit(solution)/shard_map/all_to_all | solution.py:349
  35.3 5.0 %local_mix.1 = (f32[2,128,8,128]{3,2,1,0:T(8,128)}, f32[2,128,8,128]{3,2,1,0:T(8,128)}) custom-call(bf16[1,3,128,4096]{3,2,1,0:T(8,128)(2,1)} %inputs.7, f32[9,32,128]{2,1,0:T(8,128)} %bitcast.12, bf16[4,64,16,128]{3,2,1,0:T(8,128)(2,1)S(1)} %get-tuple-element.43.gate, f32[4,32,128]{2,1,0:T(8,128)S(1)} %get-tuple-element.34.edge, f32[1,16,4096]{2,1,0:T(8,128)} %refs_2_.3, ...), custom_call_target="tpu_custom_call" | custom-call | flops 20971520 | bytes 2097152 | tf_op jit(solution)/shard_map/local_mix/pallas_call | solution.py:391
  40.3 3.8 %all-to-all-done.1.start.refs_4_ = bf16[16,32,128]{2,1,0:T(8,128)(2,1)S(1)} async-done(((bf16[16,32,128]{2,1,0:T(8,128)(2,1)}), bf16[16,32,128]{2,1,0:T(8,128)(2,1)S(1)}, u32[]{:S(2)}, u32[]{:S(2)}) %all-to-all-start.1) | async-done | bytes 131104 | tf_op jit(solution)/shard_map/all_to_all | solution.py:349
  44.1 1.8 %finished.2 = bf16[1,128,1024]{2,1,0:T(8,128)(2,1)S(1)} custom-call(f32[2,128,8,128]{3,2,1,0:T(8,128)} %get-tuple-element.45.refs_0_, f32[2,128,8,128]{3,2,1,0:T(8,128)} %get-tuple-element.46.refs_1_, f32[1,16,4096]{2,1,0:T(8,128)S(1)} %copy-done.1, f32[16,4096]{1,0:T(8,128)S(1)} %multiply_bitcast_fusion.scaled.refs_3_, ...), custom_call_target="tpu_custom_call" | custom-call | flops 3355443200 | bytes 1048576 | tf_op jit(solution)/shard_map/finished/pallas_call | solution.py:437
  45.8 0.0 collective-permute-done.2.packed
  45.8 3.4 %collective-permute-start.5 = (bf16[1,128,1024]{2,1,0:T(8,128)(2,1)S(1)}, bf16[1,128,1024]{2,1,0:T(8,128)(2,1)S(1)}, u32[]{:S(2)}, u32[]{:S(2)}) collective-permute-start(bf16[1,128,1024]{2,1,0:T(8,128)(2,1)S(1)} %finished.2), channel_id=1, source_target_pairs={{0,1},{1,2},{2,3},{3,4},{4,5},{5,6},{6,7},{7,8},{8,9},{9,10},{10,1... | collective-permute-start | bytes 786440 | tf_op jit(solution)/shard_map/ppermute | solution.py:467
  49.3 1.8 %finished.3 = bf16[1,128,1024]{2,1,0:T(8,128)(2,1)S(1)} custom-call(f32[2,128,8,128]{3,2,1,0:T(8,128)} %get-tuple-element.45.refs_0_, f32[2,128,8,128]{3,2,1,0:T(8,128)} %get-tuple-element.46.refs_1_, f32[1,16,4096]{2,1,0:T(8,128)S(1)} %copy-done.1, f32[16,4096]{1,0:T(8,128)S(1)} %multiply_bitcast_fusion.scaled.refs_3_, ...), custom_call_target="tpu_custom_call" | custom-call | flops 5242880 | bytes 1048576 | tf_op jit(solution)/shard_map/finished/pallas_call | solution.py:437
  51.1 3.1 %collective-permute-start.4 = (bf16[1,128,1024]{2,1,0:T(8,128)(2,1)S(1)}, bf16[1,128,1024]{2,1,0:T(8,128)(2,1)S(1)}, u32[]{:S(2)}, u32[]{:S(2)}) collective-permute-start(bf16[1,128,1024]{2,1,0:T(8,128)(2,1)S(1)} %finished.3), channel_id=1, source_target_pairs={{0,1},{1,2},{2,3},{3,4},{4,5},{5,6},{6,7},{7,8},{8,9},{9,10},{10,1... | collective-permute-start | bytes 786440 | tf_op jit(solution)/shard_map/ppermute | solution.py:467
  54.2 4.6 %collective-permute-start.3 = (bf16[16,8,128]{2,1,0:T(8,128)(2,1)S(1)}, bf16[16,8,128]{2,1,0:T(8,128)(2,1)S(1)}, u32[]{:S(2)}, u32[]{:S(2)}) collective-permute-start(bf16[16,8,128]{2,1,0:T(8,128)(2,1)S(1)} %fusion), channel_id=1, source_target_pairs={{0,1},{1,2},{2,3},{3,4},{4,5},{5,6},{6,7},{7,8},{8,9},{9,10},{10,1... | collective-permute-start | bytes 98312 | tf_op jit(solution)/shard_map/ppermute | solution.py:431
  58.8 2.5 %mixed_output.1 = bf16[1,128,1024]{2,1,0:T(8,128)(2,1)S(1)} custom-call(bf16[1,3,128,4096]{3,2,1,0:T(8,128)(2,1)} %inputs.7, f32[9,32,128]{2,1,0:T(8,128)} %bitcast.13, bf16[4,64,16,128]{3,2,1,0:T(8,128)(2,1)S(1)} %get-tuple-element.43.gate, f32[4,32,128]{2,1,0:T(8,128)S(1)} %get-tuple-element.34.edge, f32[1,16,4096]{2,1,0:T(8,128)} %refs_2_.3, ...), custom_call_target="tpu_custom_call" | custom-call | flops 11796480 | bytes 1048576 | tf_op jit(solution)/shard_map/mixed_output/pallas_call | solution.py:455
  61.3 3.4 %collective-permute-start.1 = (bf16[1,128,1024]{2,1,0:T(8,128)(2,1)S(1)}, bf16[1,128,1024]{2,1,0:T(8,128)(2,1)S(1)}, u32[]{:S(2)}, u32[]{:S(2)}) collective-permute-start(bf16[1,128,1024]{2,1,0:T(8,128)(2,1)S(1)} %mixed_output.1), channel_id=1, source_target_pairs={{0,1},{1,2},{2,3},{3,4},{4,5},{5,6},{6,7},{7,8},{8,9},{9,10},{10,1... | collective-permute-start | bytes 786440 | tf_op jit(solution)/shard_map/ppermute | solution.py:467
  64.8 0.5 collective-permute-done.3
  65.2 0.0 collective-permute-done.5.part
  65.2 0.7 placed.3.rest_0_
  65.9 0.0 collective-permute-done.4.part
  66.0 0.7 placed.4.rest_0_
  66.7 1.5 %finished_ahead.1.rest_0_ = bf16[1,128,4096]{2,1,0:T(8,128)(2,1)} custom-call(bf16[1,152,16,128]{3,2,1,0:T(8,128)(2,1)S(1)} %collective-permute-done.2.packed, f32[16,8,128]{2,1,0:T(8,128)S(1)} %convert_element_type.11.start, bf16[1,128,4096]{2,1,0:T(8,128)(2,1)} %placed.4.rest_0_), custom_call_target="tpu_custom_call", output_to_operand_aliasing={{}: (2, {})} | custom-call | flops 1310720000 | bytes 1048576 | tf_op jit(solution)/shard_map/finished_ahead/pallas_call | solution.py:474
  68.1 5.4 %collective-permute-done.1.part = bf16[1,128,1024]{2,1,0:T(8,128)(2,1)S(1)} collective-permute-done((bf16[1,128,1024]{2,1,0:T(8,128)(2,1)S(1)}, bf16[1,128,1024]{2,1,0:T(8,128)(2,1)S(1)}, u32[]{:S(2)}, u32[]{:S(2)}) %collective-permute-start.1) | collective-permute-done | bytes 262176 | tf_op jit(solution)/shard_map/ppermute | solution.py:467
  73.6 0.7 placed.5
  (10 shorter events, 0.1 us)
Async XLA Ops:
  0.0 7.6 %copy-start.2 = (f32[1,3,3,4096]{3,0,2,1:T(1,128)S(1)}, f32[1,3,3,4096]{3,0,2,1:T(1,128)}, u32[]{:S(2)}) copy-start(f32[1,3,3,4096]{3,0,2,1:T(1,128)} %param.6) | copy-start | bytes 442372
  0.0 20.2 %copy-start = (f32[1,16,4096]{2,1,0:T(8,128)S(1)}, f32[1,16,4096]{2,1,0:T(8,128)}, u32[]{:S(2)}) copy-start(f32[1,16,4096]{2,1,0:T(8,128)} %refs_2_.3) | copy-start | bytes 786436
  0.0 20.2 %copy-start.3 = (f32[1,16,4096]{2,1,0:T(8,128)S(1)}, f32[1,16,4096]{2,1,0:T(8,128)}, u32[]{:S(2)}) copy-start(f32[1,16,4096]{2,1,0:T(8,128)} %param.8) | copy-start | bytes 786436
  1.1 6.5 %collective-permute-start = (bf16[1,3,2,4096]{3,2,1,0:T(2,128)(2,1)S(1)}, bf16[1,3,2,4096]{3,2,1,0:T(2,128)(2,1)S(1)}, u32[]{:S(2)}, u32[]{:S(2)}) collective-permute-start(bf16[1,3,2,4096]{3,2,1,0:T(2,128)(2,1)S(1)} %slice.9), channel_id=1, source_target_pairs={{0,32},{32,64},{64,96},{96,128},{128,160},{160,192},{192,224},{224... | collective-permute-start | bytes 147464 | tf_op jit(solution)/shard_map/ppermute | solution.py:352
  8.5 20.5 %all-to-all-start = ((bf16[16,32,128]{2,1,0:T(8,128)(2,1)}), bf16[16,32,128]{2,1,0:T(8,128)(2,1)S(1)}, u32[]{:S(2)}, u32[]{:S(2)}) async-start(bf16[16,32,128]{2,1,0:T(8,128)(2,1)} %get-tuple-element.32), calls=%async_computation | async-start | bytes 262144 | tf_op jit(solution)/shard_map/all_to_all | solution.py:349
  23.8 20.2 %copy-start.1 = (f32[1,16,4096]{2,1,0:T(8,128)S(1)}, f32[1,16,4096]{2,1,0:T(8,128)}, u32[]{:S(2)}) copy-start(f32[1,16,4096]{2,1,0:T(8,128)} %refs_2_.3) | copy-start | bytes 786436
  23.8 22.0 %collective-permute-start.2 = (bf16[1,152,16,128]{3,2,1,0:T(8,128)(2,1)}, bf16[1,152,16,128]{3,2,1,0:T(8,128)(2,1)S(1)}, u32[]{:S(2)}, u32[]{:S(2)}) collective-permute-start(bf16[1,152,16,128]{3,2,1,0:T(8,128)(2,1)} %packed.1), channel_id=1, source_target_pairs={{0,1},{1,2},{2,3},{3,4},{4,5},{5,6},{6,7},{7,8},{8,9},{9,10},{10,1... | collective-permute-start | bytes 1867784 | tf_op jit(solution)/shard_map/ppermute | solution.py:417
  29.7 14.4 %all-to-all-start.1 = ((bf16[16,32,128]{2,1,0:T(8,128)(2,1)}), bf16[16,32,128]{2,1,0:T(8,128)(2,1)S(1)}, u32[]{:S(2)}, u32[]{:S(2)}) async-start(bf16[16,32,128]{2,1,0:T(8,128)(2,1)} %scan_chunks.1), calls=%async_computation.1 | async-start | bytes 262144 | tf_op jit(solution)/shard_map/all_to_all | solution.py:349
  45.8 19.4 %collective-permute-start.5 = (bf16[1,128,1024]{2,1,0:T(8,128)(2,1)S(1)}, bf16[1,128,1024]{2,1,0:T(8,128)(2,1)S(1)}, u32[]{:S(2)}, u32[]{:S(2)}) collective-permute-start(bf16[1,128,1024]{2,1,0:T(8,128)(2,1)S(1)} %finished.2), channel_id=1, source_target_pairs={{0,1},{1,2},{2,3},{3,4},{4,5},{5,6},{6,7},{7,8},{8,9},{9,10},{10,1... | collective-permute-start | bytes 786440 | tf_op jit(solution)/shard_map/ppermute | solution.py:467
  51.1 14.9 %collective-permute-start.4 = (bf16[1,128,1024]{2,1,0:T(8,128)(2,1)S(1)}, bf16[1,128,1024]{2,1,0:T(8,128)(2,1)S(1)}, u32[]{:S(2)}, u32[]{:S(2)}) collective-permute-start(bf16[1,128,1024]{2,1,0:T(8,128)(2,1)S(1)} %finished.3), channel_id=1, source_target_pairs={{0,1},{1,2},{2,3},{3,4},{4,5},{5,6},{6,7},{7,8},{8,9},{9,10},{10,1... | collective-permute-start | bytes 786440 | tf_op jit(solution)/shard_map/ppermute | solution.py:467
  54.2 11.0 %collective-permute-start.3 = (bf16[16,8,128]{2,1,0:T(8,128)(2,1)S(1)}, bf16[16,8,128]{2,1,0:T(8,128)(2,1)S(1)}, u32[]{:S(2)}, u32[]{:S(2)}) collective-permute-start(bf16[16,8,128]{2,1,0:T(8,128)(2,1)S(1)} %fusion), channel_id=1, source_target_pairs={{0,1},{1,2},{2,3},{3,4},{4,5},{5,6},{6,7},{7,8},{8,9},{9,10},{10,1... | collective-permute-start | bytes 98312 | tf_op jit(solution)/shard_map/ppermute | solution.py:431
  61.3 12.2 %collective-permute-start.1 = (bf16[1,128,1024]{2,1,0:T(8,128)(2,1)S(1)}, bf16[1,128,1024]{2,1,0:T(8,128)(2,1)S(1)}, u32[]{:S(2)}, u32[]{:S(2)}) collective-permute-start(bf16[1,128,1024]{2,1,0:T(8,128)(2,1)S(1)} %mixed_output.1), channel_id=1, source_target_pairs={{0,1},{1,2},{2,3},{3,4},{4,5},{5,6},{6,7},{7,8},{8,9},{9,10},{10,1... | collective-permute-start | bytes 786440 | tf_op jit(solution)/shard_map/ppermute | solution.py:467
